TPU v7x, 32 devices: a whole 2x2x4 slice. The times are simulated.
32 devices in a mesh: dp: 8 (over z, core), shard: 4 (over y, x).
Axes of the slice: x: 2, y: 2, z: 4, core: 2. Of those that a mesh axis runs over, the one named last changes fastest.
Arguments:
- points: bfloat16 [8192, 1024], P(('dp', 'shard'))
- first_center: bfloat16 [1024], replicated, may hold values from -0.1875 to 0.1875
- counts: int32 [3, 8, 4], P(None, 'dp', 'shard'), may hold values from 0 to 64, as said below
- cand_index: int32 [3, 8, 4, 64], P(None, 'dp', 'shard'), may hold values from 0 to 255, as said below
Outputs:
- min_dist: float32 [8192], P(('dp', 'shard'))
- weights: float32 [8192], P(('dp', 'shard'))
- potentials: float32 [4], replicated
Inputs may be any that keep to these rules, and one draw needn't show every extreme that they name: In each round the counts of the 4 devices of one dp index sum to 64, so a round has 512 candidates; in each round and dp index some device has exactly 64. `cand_index`: each device's list in a round holds distinct local row numbers; only its first counts entries are candidates.
All inputs are finite; a program needn't handle non-finite values.
Results may differ from a plain program's by a relative error of at most 0.0003.
Values may be sent and summed in bfloat16 or wider, within the bound.
A program may use at most 64 MiB of HBM per device.

v0:
```python
import jax
import jax.numpy as jnp
from jax import lax
from jax.sharding import PartitionSpec as P

CANDS_ALL = 512


def pair_dist(rows, rows_norm, cands):
    prod = jnp.dot(rows, cands.T, preferred_element_type=jnp.float32)
    cand_norm = jnp.sum(jnp.square(cands.astype(jnp.float32)), axis=1)
    return jnp.maximum(rows_norm[:, None] + cand_norm[None, :] - 2.0 * prod, 0.0)


def pack_group(group_rows, member_counts, total, stride):
    ends = jnp.cumsum(member_counts)
    begins = ends - member_counts
    slot = jnp.arange(total, dtype=jnp.int32)
    source = jnp.sum((slot[:, None] >= ends[None, :]).astype(jnp.int32), axis=1)
    offset = slot - jnp.take(begins, source)
    return jnp.take(group_rows, source * stride + offset, axis=0)


def body(points, first_center, counts, cand_index):
    rows_norm = jnp.sum(jnp.square(points.astype(jnp.float32)), axis=1)
    running = jnp.min(pair_dist(points, rows_norm, first_center[None, :]), axis=1)
    rounds = counts.shape[0]
    cap = cand_index.shape[3]
    every_count = lax.all_gather(counts.reshape(rounds, 1), ("dp", "shard"), axis=1, tiled=True)

    def global_sum(value):
        return lax.psum(value, ("dp", "shard"))

    partials = [jnp.sum(running)]
    totals = [global_sum(partials[0])]
    for step in range(rounds):
        local_rows = jnp.take(points, cand_index[step, 0, 0], axis=0)
        group_rows = lax.all_gather(local_rows, "shard", axis=0, tiled=True)
        width = lax.axis_size("shard")
        member_counts = lax.dynamic_slice_in_dim(
            every_count[step], lax.axis_index("dp") * width, width
        )
        total = CANDS_ALL // lax.axis_size("dp")
        packed = pack_group(group_rows, member_counts, total, cap)
        running = jnp.minimum(
            running,
            jnp.min(
                pair_dist(points, rows_norm, lax.all_gather(packed, "dp", axis=0, tiled=True)),
                axis=1,
            ),
        )
        partials.append(jnp.sum(running))
        totals.append(global_sum(partials[-1]))
    potentials = jnp.stack(totals)
    rows_total = points.shape[0] * lax.axis_size("dp") * lax.axis_size("shard")
    weights = running * (rows_total / potentials[-1])
    return (running, weights, potentials)


def solution(mesh):
    placed = (P(("dp", "shard"), None), P(), P(None, "dp", "shard"), P(None, "dp", "shard", None))
    return jax.shard_map(
        body,
        mesh=mesh,
        in_specs=placed,
        out_specs=(P(("dp", "shard")), P(("dp", "shard")), P()),
        check_vma=False,
    )
```

profile of v0, /device:TPU:0, one launch (start us, length us, event | category | flops | bytes accessed | tf_op | source)
XLA Modules:
  0.0 214.5 jit_solution(15320038129494646137)
XLA Ops:
  7.2 0.0 all-gather.7.cloned.1.call-start
  7.2 0.7 compare_and_fusion.5
  7.9 69.4 %all-gather = s32[3,32,1]{0,2,1:T(1,128)S(1)} all-gather(s32[3,1,1]{0,2,1:T(1,128)} %param.10), channel_id=2, replica_groups=mesh['dp'=8,'shard'=4] {'dp','shard'}, dimensions={1}, use_global_device_ids=true | all-gather | bytes 396 | tf_op jit(solution)/shard_map/all_gather | solution.py:29
  77.3 0.1 fusion.19
  77.5 1.9 gather_fusion.2
  79.4 0.1 broadcast_select_fusion.3
  79.5 0.0 copy-start
  79.5 8.7 %all_gather.24 = bf16[256,1024]{1,0:T(8,128)(2,1)S(1)} all-gather(bf16[64,1024]{1,0:T(8,128)(2,1)S(1)} %broadcast_select_fusion.3), channel_id=1, replica_groups=mesh['dp'=8,'shard'=4] {'shard'}, dimensions={0}, use_global_device_ids=true | all-gather | bytes 655360 | tf_op jit(solution)/shard_map/all_gather | solution.py:38
  88.2 0.2 dynamic-slice_reduce_fusion
  88.4 0.2 reduce-window.25
  88.6 0.6 fusion.21
  89.2 0.1 convert_reduce_fusion.1
  89.3 2.6 %compare_and_fusion.2 = (pred[64]{0:T(512)(128)(4,1)S(1)}, s32[64]{0:T(128)S(1)}) fusion(s32[]{:T(128)} %bitcast.12, s32[]{:T(128)} %bitcast.11, s32[]{:T(128)} %bitcast.10, s32[]{:T(128)} %bitcast.9, s32[64]{0:T(128)S(1)} %convert_reduce_fusion.1), kind=kLoop, calls=%fused_computation.62 | loop fusion | flops 1408 | bytes 592 | tf_op jit(solution)/shard_map/jit(_take)/and | solution.py:21
  91.9 0.7 gather_fusion.3
  92.7 0.7 broadcast_select_fusion.2
  93.4 0.0 all-gather.7.cloned.1.call-update
  93.4 0.0 all-gather.5.cloned.1.call-start
  93.5 0.0 copy-done
  93.5 0.7 gather_fusion
  94.2 0.2 dynamic-slice_reduce_fusion.2
  94.4 0.2 reduce-window.24
  94.5 0.1 broadcast_select_fusion.5
  94.6 10.6 %all_gather.21 = bf16[256,1024]{1,0:T(8,128)(2,1)S(1)} all-gather(bf16[64,1024]{1,0:T(8,128)(2,1)S(1)} %broadcast_select_fusion.5), channel_id=1, replica_groups=mesh['dp'=8,'shard'=4] {'shard'}, dimensions={0}, use_global_device_ids=true | all-gather | bytes 655360 | tf_op jit(solution)/shard_map/all_gather | solution.py:38
  105.2 0.6 fusion.20
  105.8 0.1 convert_reduce_fusion.2
  105.9 2.6 %compare_and_fusion.4 = (pred[64]{0:T(512)(128)(4,1)S(1)}, s32[64]{0:T(128)S(1)}) fusion(s32[]{:T(128)} %bitcast.5, s32[]{:T(128)} %bitcast.4, s32[]{:T(128)} %bitcast.3, s32[]{:T(128)} %bitcast.2, s32[64]{0:T(128)S(1)} %convert_reduce_fusion.2), kind=kLoop, calls=%fused_computation.68 | loop fusion | flops 1408 | bytes 592 | tf_op jit(solution)/shard_map/jit(_take)/and | solution.py:21
  108.5 0.7 gather_fusion.1
  109.3 0.7 broadcast_select_fusion.4
  110.0 0.0 all-gather.5.cloned.1.call-update
  110.0 0.0 all-gather.9.cloned.1.call-start
  110.1 0.7 gather_fusion.4
  110.8 0.2 reduce-window.26
  111.0 0.1 broadcast_select_fusion.1
  111.1 0.0 copy-start.4
  111.1 8.5 %all_gather.26 = bf16[256,1024]{1,0:T(8,128)(2,1)S(1)} all-gather(bf16[64,1024]{1,0:T(8,128)(2,1)S(1)} %broadcast_select_fusion.1), channel_id=1, replica_groups=mesh['dp'=8,'shard'=4] {'shard'}, dimensions={0}, use_global_device_ids=true | all-gather | bytes 655360 | tf_op jit(solution)/shard_map/all_gather | solution.py:38
  119.6 0.6 fusion.22
  120.2 0.1 convert_reduce_fusion
  120.3 2.5 %compare_and_fusion = (pred[64]{0:T(512)(128)(4,1)S(1)}, s32[64]{0:T(128)S(1)}) fusion(s32[]{:T(128)} %bitcast.19, s32[]{:T(128)} %bitcast.18, s32[]{:T(128)} %bitcast.17, s32[]{:T(128)} %bitcast.16, s32[64]{0:T(128)S(1)} %convert_reduce_fusion), kind=kLoop, calls=%fused_computation.56 | loop fusion | flops 1408 | bytes 592 | tf_op jit(solution)/shard_map/jit(_take)/and | solution.py:21
  122.8 0.7 gather_fusion.5
  123.5 0.7 broadcast_select_fusion
  124.3 0.0 all-gather.9.cloned.1.call-update
  124.3 0.0 copy-done.4
  124.3 0.6 multiply_reduce_fusion.4
  124.9 0.2 multiply_reduce_fusion.3
  125.1 0.2 fusion.23
  125.3 0.0 all-gather.7.cloned.1.call-done
  125.3 1.6 multiply_reduce_fusion.1
  126.9 9.9 %all-gather.5.cloned.1.call-done = bf16[512,1024]{1,0:T(8,128)(2,1)} async-done(((bf16[64,1024]{1,0:T(8,128)(2,1)}), bf16[512,1024]{1,0:T(8,128)(2,1)}) %all-gather.5.cloned.1.call-update) | async-done | bytes 1048592 | tf_op jit(solution)/shard_map/all_gather | solution.py:48
  136.8 1.5 multiply_reduce_fusion.2
  138.3 0.0 copy-done.1
  138.3 0.0 copy-start.2
  138.3 0.5 fusion.10
  138.8 0.7 copy-done.2
  139.6 0.5 fusion.9
  140.1 1.3 minimum_reduce_fusion.1
  141.3 18.9 %all-gather.9.cloned.1.call-done = bf16[512,1024]{1,0:T(8,128)(2,1)} async-done(((bf16[64,1024]{1,0:T(8,128)(2,1)}), bf16[512,1024]{1,0:T(8,128)(2,1)}) %all-gather.9.cloned.1.call-update) | async-done | bytes 1048592 | tf_op jit(solution)/shard_map/all_gather | solution.py:48
  160.2 1.6 multiply_reduce_fusion
  161.8 0.0 copy-done.3
  161.8 0.5 fusion.11
  162.3 0.6 fusion.18
  162.9 40.7 %all-reduce = (f32[]{:T(128)}, f32[1]{0:T(128)}, f32[1]{0:T(128)}, f32[1]{0:T(128)}) all-reduce(f32[]{:T(128)} %get-tuple-element.13, f32[1]{0:T(128)} %bitcast.24, f32[1]{0:T(128)} %bitcast.23, f32[1]{0:T(128)} %bitcast.22), channel_id=1, replica_groups=mesh['dp'=8,'shard'=4] {'dp','shard'}, use_global_device_ids=true, to_apply=%region_15.18 | all-reduce | flops 4 | bytes 32 | tf_op jit(solution)/shard_map/psum | solution.py:32
  204.3 0.6 broadcast_multiply_fusion
  204.9 3.1 %pad_maximum_fusion = f32[4]{0:T(128)} fusion(f32[1]{0:T(128)} %bitcast.25, f32[1]{0:T(128)} %get-tuple-element.9, f32[1]{0:T(128)} %get-tuple-element.10, f32[1]{0:T(128)} %get-tuple-element.11), kind=kLoop, calls=%fused_computation.81 | loop fusion | flops 12 | bytes 32 | tf_op jit(solution)/shard_map/stack | solution.py:54
  208.0 0.0 copy-done.5
  (13 shorter events, 0.1 us)
Async XLA Ops:
  7.2 118.2 %all-gather.7.cloned.1.call-start = ((), (), s32[]{:S(2)}) async-start(), calls=%async_computation.1 | async-start | bytes 1179648 | tf_op jit(solution)/shard_map/all_gather | solution.py:48
  79.5 14.0 %copy-start = (bf16[256,1024]{1,0:T(8,128)(2,1)S(1)}, bf16[256,1024]{1,0:T(8,128)(2,1)}, u32[]{:S(2)}) copy-start(bf16[256,1024]{1,0:T(8,128)(2,1)} %param.8) | copy-start | bytes 1572868
  93.4 43.4 %all-gather.5.cloned.1.call-start = ((), (), s32[]{:S(2)}) async-start(), calls=%async_computation | async-start | bytes 1179648 | tf_op jit(solution)/shard_map/all_gather | solution.py:48
  110.0 50.2 %all-gather.9.cloned.1.call-start = ((), (), s32[]{:S(2)}) async-start(), calls=%async_computation.2 | async-start | bytes 1179648 | tf_op jit(solution)/shard_map/all_gather | solution.py:48
  111.1 13.2 %copy-start.4 = (bf16[1024]{0:T(1024)(128)(2,1)S(1)}, bf16[1024]{0:T(1024)(128)(2,1)}, u32[]{:S(2)}) copy-start(bf16[1024]{0:T(1024)(128)(2,1)} %param.9) | copy-start | bytes 6148
  125.3 13.0 %copy-start.1 = (bf16[512,1024]{1,0:T(8,128)(2,1)S(1)}, bf16[512,1024]{1,0:T(8,128)(2,1)}, u32[]{:S(2)}) copy-start(bf16[512,1024]{1,0:T(8,128)(2,1)} %all-gather.7.cloned.1.call-done) | copy-start | bytes 3145732
  138.3 1.2 copy-start.2
  160.2 1.6 copy-start.3
  162.9 45.1 %copy-start.5 = (f32[256]{0:T(256)}, f32[256]{0:T(256)S(1)}, u32[]{:S(2)}) copy-start(f32[256]{0:T(256)S(1)} %get-tuple-element.14) | copy-start | bytes 3076
Sparse Core Ops, SparseCore 0:
  93.5 19.8 all-gather.6
  115.1 21.7 all-gather.4
  138.4 21.6 all-gather.8
where the time goes:
time: 215 us
  blocking collectives  138 us (64%)
  waiting for transfers between devices  28.8 us (13%)
  other arithmetic  22.8 us (11%)
  between operations  14.7 us (7%)
  local copies, waits for them, and re-layouts  8.51 us (4%)
    all_gather x1, blocking collectives, body(): lax.all_gather(counts.reshape(rounds, 1), ('dp', 'shard'), axis=1, tiled=...  69.4 us
    psum x1, blocking collectives, global_sum(): return lax.psum(value, ('dp', 'shard'))  40.7 us
    all_gather x3, waiting for transfers between devices, body(): lax.all_gather(packed, 'dp', axis=0, tiled=True)  28.7 us
    all_gather x3, blocking collectives, body(): group_rows = lax.all_gather(local_rows, 'shard', axis=0, tiled=True)  27.8 us
    and x3, other arithmetic, pack_group(): return jnp.take(group_rows, source * stride + offset, axis=0)  7.81 us
    reduce_sum x4, other arithmetic, pair_dist(): cand_norm = jnp.sum(jnp.square(cands.astype(jnp.float32)), axis=1)  5.31 us
  transfers between devices with their start and end apart: 3, of which 2 were waited for; matrix products, arithmetic and copies ran while one was open for 8% of the time, Pallas kernels for 0%

commit v1 on v0

--- a/solution.py
+++ b/solution.py
@@ -1,9 +1,354 @@
+import functools
+
 import jax
 import jax.numpy as jnp
 from jax import lax
+from jax.experimental import pallas as pl
+from jax.experimental.pallas import tpu as pltpu
 from jax.sharding import PartitionSpec as P
 
 CANDS_ALL = 512
+QUAD = 4
+TILE_ROWS = 16
+LANES = 128
+MESH = pl.DeviceIdType.MESH
+CONTRACT_LAST = (((1,), (1,)), ((), ()))
+CONTRACT_FIRST = (((0,), (0,)), ((), ()))
+
+
+def round_kernel(
+    groups,
+    width,
+    pts_hbm,
+    fc_ref,
+    cnt_ref,
+    idx_ref,
+    run_ref,
+    wgt_ref,
+    pot_ref,
+    pts,
+    packed,
+    parts,
+    cand,
+    least_out,
+    least_in,
+    plane_sums,
+    dp_sums,
+    local_sem,
+    part_send,
+    part_recv,
+    plane_send,
+    plane_recv,
+    class_send,
+    class_recv,
+    core_send,
+    core_recv,
+    z_send,
+    z_recv,
+    fwd_send,
+    fwd_recv,
+    least_send,
+    least_recv,
+    psum_send,
+    psum_recv,
+    dsum_send,
+    dsum_recv,
+):
+    rounds, total = idx_ref.shape
+    rows, depth = pts_hbm.shape
+    each = total // width
+    classes = groups // QUAD
+    chunks = z_send.shape[0]
+    chunk = rows // chunks
+
+    dp, me = lax.axis_index("dp"), lax.axis_index("shard")
+    cls, mine = dp // QUAD, dp % QUAD
+    zside, core = mine // 2, mine % 2
+    partner = zside * 2 + (1 - core)
+    across = (1 - zside) * 2 + core
+    diagonal = (1 - zside) * 2 + (1 - core)
+
+    def copy(src, dst, send, recv, to):
+        made = pltpu.make_async_remote_copy(
+            src_ref=src, dst_ref=dst, send_sem=send, recv_sem=recv, device_id=to, device_id_type=MESH
+        )
+        made.start()
+        sent.append(made)
+
+    def arrived(dst, send, recv):
+        pltpu.make_async_remote_copy(
+            src_ref=dst,
+            dst_ref=dst,
+            send_sem=send,
+            recv_sem=recv,
+            device_id=(dp, lax.rem(me + 1, width)),
+            device_id_type=MESH,
+        ).wait_recv()
+
+    sent = []
+    in_quad = lambda k: (cls * QUAD + k, me)
+    in_plane = lambda off: (dp, lax.rem(me + off, width))
+    in_dp = lambda off: (lax.rem(dp + off, groups), me)
+    in_class = lambda off: (lax.rem(dp + off * QUAD, groups), me)
+
+    load = pltpu.make_async_copy(pts_hbm, pts.at[mine], local_sem)
+    load.start()
+    barrier = pltpu.get_barrier_semaphore()
+    for off in range(1, width):
+        pl.semaphore_signal(barrier, inc=1, device_id=in_plane(off), device_id_type=MESH)
+    for off in range(1, groups):
+        pl.semaphore_signal(barrier, inc=1, device_id=in_dp(off), device_id_type=MESH)
+    load.wait()
+
+    def pick(t):
+        spot = lax.broadcasted_iota(jnp.int32, (rows, total), 0)
+        slot = lax.broadcasted_iota(jnp.int32, (rows, total), 1)
+        hit = (spot == idx_ref[t : t + 1, :]) & (slot < cnt_ref[t : t + 1, :])
+        chosen = lax.dot_general(
+            jnp.where(hit, 1.0, 0.0).astype(pts.dtype),
+            pts[mine],
+            CONTRACT_FIRST,
+            preferred_element_type=jnp.float32,
+        )
+        packed[t] = chosen.astype(packed.dtype).reshape(width, each, depth)
+
+    def scatter(t):
+        for off in range(1, width):
+            copy(
+                packed.at[t, lax.rem(me + off, width)],
+                parts.at[t, me],
+                part_send.at[t, off - 1],
+                part_recv.at[t, off - 1],
+                in_plane(off),
+            )
+
+    pick(0)
+    pl.semaphore_wait(barrier, width - 1 + groups - 1)
+    scatter(0)
+    for j in range(chunks):
+        span = pl.ds(j * chunk, chunk)
+        copy(pts_hbm.at[span], pts.at[mine, span], z_send.at[j], z_recv.at[j], in_quad(across))
+    for t in range(1, rounds):
+        pick(t)
+        scatter(t)
+    copy(pts_hbm, pts.at[mine], core_send, core_recv, in_quad(partner))
+
+    squares = jnp.square(pts[mine].astype(jnp.float32))
+    lanes = squares[:, :LANES]
+    for j in range(1, depth // LANES):
+        lanes = lanes + squares[:, j * LANES : (j + 1) * LANES]
+    rows_norm = jnp.sum(lanes.T, axis=0, keepdims=True)
+    first = fc_ref[...]
+    first_norm = jnp.sum(jnp.square(first.astype(jnp.float32)), axis=1, keepdims=True)
+    first_prod = lax.dot_general(
+        jnp.broadcast_to(first, (TILE_ROWS, depth)),
+        pts[mine],
+        CONTRACT_LAST,
+        preferred_element_type=jnp.float32,
+    )[:1]
+    running = jnp.maximum(rows_norm + first_norm - 2.0 * first_prod, 0.0)
+
+    def spread(t, c, at):
+        for off in range(1, width):
+            copy(
+                cand.at[t, c, me],
+                cand.at[t, c, me],
+                plane_send.at[t, at, off - 1],
+                plane_recv.at[t, at, off - 1],
+                in_plane(off),
+            )
+
+    for t in range(rounds):
+        held = packed[t, me].astype(jnp.float32)
+        for off in range(1, width):
+            source = lax.rem(me - off + width, width)
+            arrived(parts.at[t, source], part_send.at[t, off - 1], part_recv.at[t, off - 1])
+            held = held + parts[t, source].astype(jnp.float32)
+        cand[t, cls, me] = held.astype(cand.dtype)
+        for off in range(1, classes):
+            copy(
+                cand.at[t, cls, me],
+                cand.at[t, cls, me],
+                class_send.at[t, off - 1],
+                class_recv.at[t, off - 1],
+                in_class(off),
+            )
+        spread(t, cls, 0)
+    for t in range(rounds):
+        for off in range(1, classes):
+            source = lax.rem(cls - off + classes, classes)
+            arrived(cand.at[t, source, me], class_send.at[t, off - 1], class_recv.at[t, off - 1])
+            spread(t, source, off)
+
+    norms = []
+
+    def centers(t):
+        return cand[t].reshape(classes * width * each, depth)
+
+    def least(t, k, lo, size):
+        prod = lax.dot_general(
+            centers(t), pts[k, lo : lo + size], CONTRACT_LAST, preferred_element_type=jnp.float32
+        )
+        least_out[k, t : t + 1, lo : lo + size] = jnp.min(
+            norms[t] - 2.0 * prod, axis=0, keepdims=True
+        )
+
+    def give(k, at):
+        copy(least_out.at[k], least_in.at[mine], least_send.at[at], least_recv.at[at], in_quad(k))
+
+    least_out[...] = jnp.zeros_like(least_out)
+    arrived(pts.at[partner], core_send, core_recv)
+    for t in range(rounds):
+        for at in range(classes):
+            c = lax.rem(cls - at + classes, classes)
+            for off in range(1, width):
+                source = lax.rem(me - off + width, width)
+                arrived(
+                    cand.at[t, c, source],
+                    plane_send.at[t, at, off - 1],
+                    plane_recv.at[t, at, off - 1],
+                )
+        norms.append(
+            jnp.sum(jnp.square(centers(t).astype(jnp.float32)), axis=1, keepdims=True)
+        )
+        least(t, mine, 0, rows)
+        least(t, partner, 0, rows)
+    give(partner, 0)
+    for j in range(chunks):
+        span = pl.ds(j * chunk, chunk)
+        arrived(pts.at[across, span], z_send.at[j], z_recv.at[j])
+        copy(
+            pts.at[across, span], pts.at[across, span], fwd_send.at[j], fwd_recv.at[j], in_quad(partner)
+        )
+        for t in range(rounds):
+            least(t, across, j * chunk, chunk)
+    give(across, 1)
+    for j in range(chunks):
+        arrived(pts.at[diagonal, pl.ds(j * chunk, chunk)], fwd_send.at[j], fwd_recv.at[j])
+        for t in range(rounds):
+            least(t, diagonal, j * chunk, chunk)
+    give(diagonal, 2)
+
+    near = least_out[mine]
+    for at, k in enumerate((partner, across, diagonal)):
+        arrived(least_in.at[k], least_send.at[at], least_recv.at[at])
+        near = jnp.minimum(near, least_in[k])
+
+    def fold(row):
+        out = row[:, :LANES]
+        for j in range(1, rows // LANES):
+            out = out + row[:, j * LANES : (j + 1) * LANES]
+        return out
+
+    partials = [fold(running)]
+    for t in range(rounds):
+        running = jnp.minimum(running, jnp.maximum(rows_norm + near[t : t + 1], 0.0))
+        partials.append(fold(running))
+    run_ref[...] = running
+
+    tall = plane_sums.shape[1]
+    partials += [jnp.zeros_like(partials[0])] * (tall - len(partials))
+    plane_sums[me] = jnp.concatenate(partials, axis=0)
+    for off in range(1, width):
+        copy(
+            plane_sums.at[me],
+            plane_sums.at[me],
+            psum_send.at[off - 1],
+            psum_recv.at[off - 1],
+            in_plane(off),
+        )
+    for off in range(1, width):
+        source = lax.rem(me - off + width, width)
+        arrived(plane_sums.at[source], psum_send.at[off - 1], psum_recv.at[off - 1])
+    dp_sums[dp] = jnp.sum(plane_sums[...], axis=0)
+    for off in range(1, groups):
+        copy(
+            dp_sums.at[dp], dp_sums.at[dp], dsum_send.at[off - 1], dsum_recv.at[off - 1], in_dp(off)
+        )
+    for off in range(1, groups):
+        source = lax.rem(dp - off + groups, groups)
+        arrived(dp_sums.at[source], dsum_send.at[off - 1], dsum_recv.at[off - 1])
+    sums = jnp.sum(jnp.sum(dp_sums[...], axis=0), axis=1, keepdims=True)
+    rows_all = rows * groups * width
+    wgt_ref[...] = running * (rows_all / sums[rounds : rounds + 1])
+    for t in range(rounds + 1):
+        pot_ref[t] = sums[t, 0]
+    for made in sent:
+        made.wait_send()
+
+
+def fused(points, first_center, counts, cand_index):
+    rows, depth = points.shape
+    rounds, total = counts.shape[0], cand_index.shape[3]
+    groups, width = lax.axis_size("dp"), lax.axis_size("shard")
+    each, classes = total // width, groups // QUAD
+    chunks, tall = 2, 8
+    f32, held = jnp.float32, points.dtype
+    dma = pltpu.SemaphoreType.DMA
+    vmem = pl.BlockSpec(memory_space=pltpu.VMEM)
+    running, weights, potentials = pl.pallas_call(
+        functools.partial(round_kernel, groups, width),
+        out_shape=(
+            jax.ShapeDtypeStruct((1, rows), f32),
+            jax.ShapeDtypeStruct((1, rows), f32),
+            jax.ShapeDtypeStruct((rounds + 1,), f32),
+        ),
+        in_specs=[pl.BlockSpec(memory_space=pl.ANY), vmem, vmem, vmem],
+        out_specs=(vmem, vmem, pl.BlockSpec(memory_space=pltpu.SMEM)),
+        scratch_shapes=[
+            pltpu.VMEM((QUAD, rows, depth), held),
+            pltpu.VMEM((rounds, width, each, depth), held),
+            pltpu.VMEM((rounds, width, each, depth), held),
+            pltpu.VMEM((rounds, classes, width, each, depth), held),
+            pltpu.VMEM((QUAD, tall, rows), f32),
+            pltpu.VMEM((QUAD, tall, rows), f32),
+            pltpu.VMEM((width, tall, LANES), f32),
+            pltpu.VMEM((groups, tall, LANES), f32),
+            dma,
+            dma((rounds, width - 1)),
+            dma((rounds, width - 1)),
+            dma((rounds, classes, width - 1)),
+            dma((rounds, classes, width - 1)),
+            dma((rounds, max(classes - 1, 1))),
+            dma((rounds, max(classes - 1, 1))),
+            dma,
+            dma,
+            dma((chunks,)),
+            dma((chunks,)),
+            dma((chunks,)),
+            dma((chunks,)),
+            dma((QUAD - 1,)),
+            dma((QUAD - 1,)),
+            dma((width - 1,)),
+            dma((width - 1,)),
+            dma((groups - 1,)),
+            dma((groups - 1,)),
+        ],
+        compiler_params=pltpu.CompilerParams(
+            collective_id=0, has_side_effects=True, vmem_limit_bytes=40 * 1024 * 1024
+        ),
+    )(
+        points,
+        first_center.reshape(1, depth),
+        counts.reshape(rounds, 1),
+        cand_index.reshape(rounds, total),
+    )
+    return running.reshape(rows), weights.reshape(rows), potentials
+
+
+def one_holder(points, counts, cand_index):
+    rows, depth = points.shape
+    groups, width = lax.axis_size("dp"), lax.axis_size("shard")
+    total = CANDS_ALL // groups
+    return (
+        cand_index.shape[3] == total
+        and groups % QUAD == 0
+        and width > 1
+        and total % (width * TILE_ROWS) == 0
+        and rows % (2 * LANES) == 0
+        and depth % LANES == 0
+        and counts.shape[0] < 8
+    )
 
 
 def pair_dist(rows, rows_norm, cands):
@@ -21,7 +366,7 @@
     return jnp.take(group_rows, source * stride + offset, axis=0)
 
 
-def body(points, first_center, counts, cand_index):
+def separate(points, first_center, counts, cand_index):
     rows_norm = jnp.sum(jnp.square(points.astype(jnp.float32)), axis=1)
     running = jnp.min(pair_dist(points, rows_norm, first_center[None, :]), axis=1)
     rounds = counts.shape[0]
@@ -55,6 +400,12 @@
     rows_total = points.shape[0] * lax.axis_size("dp") * lax.axis_size("shard")
     weights = running * (rows_total / potentials[-1])
     return (running, weights, potentials)
+
+
+def body(points, first_center, counts, cand_index):
+    if one_holder(points, counts, cand_index):
+        return fused(points, first_center, counts, cand_index)
+    return separate(points, first_center, counts, cand_index)
 
 
 def solution(mesh):

time: 215 us -> 44.5 us (0.21)
  blocking collectives: 138 us -> 0 us
  Pallas kernels: 0 us -> 39 us
  waiting for transfers between devices: 28.8 us -> 0 us
  other arithmetic: 22.8 us -> 0 us
  between operations: 14.7 us -> 0.65 us
  local copies, waits for them, and re-layouts: 8.51 us -> 4.69 us
    all_gather x4 -> x0, blocking collectives: 97.2 us -> none  [the longest x1 69.4 us: body(): lax.all_gather(counts.reshape(rounds, 1), ('dp', 'shard'), axis=1, tiled=...]
    psum x1 -> x0, blocking collectives: 40.7 us -> none  [global_sum(): return lax.psum(value, ('dp', 'shard'))]
    pallas_call x0 -> x1, Pallas kernels: none -> 39 us  [fused(): pl.pallas_call(functools.partial(round_kernel, groups, width), out_shape=...]
    all_gather x3 -> x0, waiting for transfers between devices: 28.7 us -> none  [body(): lax.all_gather(packed, 'dp', axis=0, tiled=True)]
    and x4 -> x0, other arithmetic: 8.5 us -> none  [the longest x3 7.81 us: pack_group(): return jnp.take(group_rows, source * stride + offset, axis=0)]
    reduce_sum x10 -> x0, other arithmetic: 7.62 us -> none  [the longest x4 5.31 us: pair_dist(): cand_norm = jnp.sum(jnp.square(cands.astype(jnp.float32)), axis=1)]
    gather x9 -> x0, local copies, waits for them, and re-layouts: 7.24 us -> none  [the longest x3 3.32 us: body(): local_rows = jnp.take(points, cand_index[step, 0, 0], axis=0)]
    unnamed x13 -> x12, local copies, waits for them, and re-layouts: 0.75 us -> 4.6 us
  transfers between devices with their start and end apart: 3 -> 0, of which waited for: 2 -> 0; matrix products, arithmetic and copies ran while one was open for 8% -> 0% of each run, Pallas kernels for 0% -> 0%
where the time goes in v1:
time: 44.5 us; the launch traced here: 44.3 us
  Pallas kernels  39 us (88%)
  local copies, waits for them, and re-layouts  4.69 us (11%)
  between operations  0.65 us (1%)
    pallas_call x1, Pallas kernels, fused(): pl.pallas_call(functools.partial(round_kernel, groups, width), out_shape=...  39 us
    unnamed x12, local copies, waits for them, and re-layouts  4.6 us

profile of v1, /device:TPU:0, one launch (start us, length us, event | category | flops | bytes accessed | tf_op | source)
XLA Modules:
  0.0 44.3 jit_solution(4757837410260522058)
XLA Ops:
  0.6 0.0 copy-start.3
  0.6 0.6 %copy-done.3 = s32[3,1,1]{0,2,1:T(1,128)S(1)} copy-done((s32[3,1,1]{0,2,1:T(1,128)S(1)}, s32[3,1,1]{0,2,1:T(1,128)}, u32[]{:S(2)}) %copy-start.3) | copy-done | bytes 36
  1.3 0.0 copy-start.2
  1.3 0.1 copy.7.cnt_ref
  1.4 0.6 %copy-done.2 = s32[3,1,1,64]{3,2,1,0:T(1,128)S(1)} copy-done((s32[3,1,1,64]{3,2,1,0:T(1,128)S(1)}, s32[3,1,1,64]{3,2,1,0:T(1,128)}, u32[]{:S(2)}) %copy-start.2) | copy-done | bytes 792
  2.0 0.0 copy-start.1
  2.0 0.7 %copy-done.1 = bf16[1024]{0:T(1024)(128)(2,1)S(1)} copy-done((bf16[1024]{0:T(1024)(128)(2,1)S(1)}, bf16[1024]{0:T(1024)(128)(2,1)}, u32[]{:S(2)}) %copy-start.1) | copy-done | bytes 2072
  2.7 0.0 copy-start
  2.7 1.0 %copy-done = bf16[256,1024]{1,0:T(8,128)(2,1)S(1)} copy-done((bf16[256,1024]{1,0:T(8,128)(2,1)S(1)}, bf16[256,1024]{1,0:T(8,128)(2,1)}, u32[]{:S(2)}) %copy-start) | copy-done | bytes 524312
  3.7 39.0 %shard_map.67 = (f32[1,256]{1,0:T(1,128)S(1)}, f32[1,256]{1,0:T(1,128)S(1)}, f32[4]{0:T(128)S(1)}) custom-call(bf16[256,1024]{1,0:T(8,128)(2,1)S(1)} %copy-done, bf16[1,1024]{1,0:T(2,128)(2,1)S(1)} %reshape.21.fc_ref, s32[3,1]{1,0:T(4,128)S(1)} %copy.7.cnt_ref, s32[3,64]{1,0:T(4,128)S(1)} %bitcast.6), custom_call_target="tpu_custom_call" | custom-call | tf_op jit(solution)/shard_map/pallas_call | solution.py:289
  42.7 0.6 %copy.14 = f32[256]{0:T(256)} copy(f32[256]{0:T(256)S(1)} %bitcast.8) | data formatting | bytes 2048
  43.2 0.6 %copy.15 = f32[256]{0:T(256)} copy(f32[256]{0:T(256)S(1)} %bitcast.7) | data formatting | bytes 2048
  43.8 0.5 %copy.16 = f32[4]{0:T(128)} copy(f32[4]{0:T(128)S(1)} %get-tuple-element.14) | data formatting | bytes 32
  (2 shorter events, 0.0 us)
Async XLA Ops:
  0.6 0.7 %copy-start.3 = (s32[3,1,1]{0,2,1:T(1,128)S(1)}, s32[3,1,1]{0,2,1:T(1,128)}, u32[]{:S(2)}) copy-start(s32[3,1,1]{0,2,1:T(1,128)} %param.6) | copy-start | bytes 40
  1.3 0.7 %copy-start.2 = (s32[3,1,1,64]{3,2,1,0:T(1,128)S(1)}, s32[3,1,1,64]{3,2,1,0:T(1,128)}, u32[]{:S(2)}) copy-start(s32[3,1,1,64]{3,2,1,0:T(1,128)} %param.7) | copy-start | bytes 2308
  2.0 0.7 %copy-start.1 = (bf16[1024]{0:T(1024)(128)(2,1)S(1)}, bf16[1024]{0:T(1024)(128)(2,1)}, u32[]{:S(2)}) copy-start(bf16[1024]{0:T(1024)(128)(2,1)} %param.5) | copy-start | bytes 6148
  2.7 1.0 %copy-start = (bf16[256,1024]{1,0:T(8,128)(2,1)S(1)}, bf16[256,1024]{1,0:T(8,128)(2,1)}, u32[]{:S(2)}) copy-start(bf16[256,1024]{1,0:T(8,128)(2,1)} %pts_hbm.1) | copy-start | bytes 1572868

commit v2 on v1

--- a/solution.py
+++ b/solution.py
@@ -20,12 +20,13 @@
     groups,
     width,
     pts_hbm,
+    fc_hbm,
+    cnt_hbm,
+    idx_hbm,
+    out_ref,
     fc_ref,
     cnt_ref,
     idx_ref,
-    run_ref,
-    wgt_ref,
-    pot_ref,
     pts,
     packed,
     parts,
@@ -34,7 +35,7 @@
     least_in,
     plane_sums,
     dp_sums,
-    local_sem,
+    local_sems,
     part_send,
     part_recv,
     plane_send,
@@ -54,7 +55,7 @@
     dsum_send,
     dsum_recv,
 ):
-    rounds, total = idx_ref.shape
+    rounds, total = idx_ref.shape[0], idx_ref.shape[3]
     rows, depth = pts_hbm.shape
     each = total // width
     classes = groups // QUAD
@@ -91,19 +92,31 @@
     in_dp = lambda off: (lax.rem(dp + off, groups), me)
     in_class = lambda off: (lax.rem(dp + off * QUAD, groups), me)
 
-    load = pltpu.make_async_copy(pts_hbm, pts.at[mine], local_sem)
-    load.start()
+    loads = [
+        pltpu.make_async_copy(src, dst, local_sems.at[j])
+        for j, (src, dst) in enumerate(
+            (
+                (idx_hbm, idx_ref),
+                (cnt_hbm, cnt_ref),
+                (pts_hbm, pts.at[mine]),
+                (fc_hbm, fc_ref),
+            )
+        )
+    ]
+    for load in loads:
+        load.start()
     barrier = pltpu.get_barrier_semaphore()
     for off in range(1, width):
         pl.semaphore_signal(barrier, inc=1, device_id=in_plane(off), device_id_type=MESH)
     for off in range(1, groups):
         pl.semaphore_signal(barrier, inc=1, device_id=in_dp(off), device_id_type=MESH)
-    load.wait()
+    for load in loads:
+        load.wait()
 
     def pick(t):
         spot = lax.broadcasted_iota(jnp.int32, (rows, total), 0)
         slot = lax.broadcasted_iota(jnp.int32, (rows, total), 1)
-        hit = (spot == idx_ref[t : t + 1, :]) & (slot < cnt_ref[t : t + 1, :])
+        hit = (spot == idx_ref[t, 0]) & (slot < cnt_ref[t])
         chosen = lax.dot_general(
             jnp.where(hit, 1.0, 0.0).astype(pts.dtype),
             pts[mine],
@@ -125,9 +138,12 @@
     pick(0)
     pl.semaphore_wait(barrier, width - 1 + groups - 1)
     scatter(0)
-    for j in range(chunks):
+
+    def cross(j):
         span = pl.ds(j * chunk, chunk)
         copy(pts_hbm.at[span], pts.at[mine, span], z_send.at[j], z_recv.at[j], in_quad(across))
+
+    cross(0)
     for t in range(1, rounds):
         pick(t)
         scatter(t)
@@ -138,7 +154,7 @@
     for j in range(1, depth // LANES):
         lanes = lanes + squares[:, j * LANES : (j + 1) * LANES]
     rows_norm = jnp.sum(lanes.T, axis=0, keepdims=True)
-    first = fc_ref[...]
+    first = fc_ref[...].reshape(1, depth)
     first_norm = jnp.sum(jnp.square(first.astype(jnp.float32)), axis=1, keepdims=True)
     first_prod = lax.dot_general(
         jnp.broadcast_to(first, (TILE_ROWS, depth)),
@@ -174,6 +190,8 @@
                 in_class(off),
             )
         spread(t, cls, 0)
+        for j in range(1 + t * (chunks - 1) // rounds, 1 + (t + 1) * (chunks - 1) // rounds):
+            cross(j)
     for t in range(rounds):
         for off in range(1, classes):
             source = lax.rem(cls - off + classes, classes)
@@ -214,19 +232,25 @@
         least(t, mine, 0, rows)
         least(t, partner, 0, rows)
     give(partner, 0)
-    for j in range(chunks):
-        span = pl.ds(j * chunk, chunk)
-        arrived(pts.at[across, span], z_send.at[j], z_recv.at[j])
-        copy(
-            pts.at[across, span], pts.at[across, span], fwd_send.at[j], fwd_recv.at[j], in_quad(partner)
-        )
+    for lo in range(0, rows, LANES):
+        for j in range(lo // chunk, (lo + LANES) // chunk):
+            span = pl.ds(j * chunk, chunk)
+            arrived(pts.at[across, span], z_send.at[j], z_recv.at[j])
+            copy(
+                pts.at[across, span],
+                pts.at[across, span],
+                fwd_send.at[j],
+                fwd_recv.at[j],
+                in_quad(partner),
+            )
         for t in range(rounds):
-            least(t, across, j * chunk, chunk)
+            least(t, across, lo, LANES)
     give(across, 1)
-    for j in range(chunks):
-        arrived(pts.at[diagonal, pl.ds(j * chunk, chunk)], fwd_send.at[j], fwd_recv.at[j])
+    for lo in range(0, rows, LANES):
+        for j in range(lo // chunk, (lo + LANES) // chunk):
+            arrived(pts.at[diagonal, pl.ds(j * chunk, chunk)], fwd_send.at[j], fwd_recv.at[j])
         for t in range(rounds):
-            least(t, diagonal, j * chunk, chunk)
+            least(t, diagonal, lo, LANES)
     give(diagonal, 2)
 
     near = least_out[mine]
@@ -244,7 +268,7 @@
     for t in range(rounds):
         running = jnp.minimum(running, jnp.maximum(rows_norm + near[t : t + 1], 0.0))
         partials.append(fold(running))
-    run_ref[...] = running
+    out_ref[0:1] = running
 
     tall = plane_sums.shape[1]
     partials += [jnp.zeros_like(partials[0])] * (tall - len(partials))
@@ -270,9 +294,10 @@
         arrived(dp_sums.at[source], dsum_send.at[off - 1], dsum_recv.at[off - 1])
     sums = jnp.sum(jnp.sum(dp_sums[...], axis=0), axis=1, keepdims=True)
     rows_all = rows * groups * width
-    wgt_ref[...] = running * (rows_all / sums[rounds : rounds + 1])
-    for t in range(rounds + 1):
-        pot_ref[t] = sums[t, 0]
+    out_ref[1:2] = running * (rows_all / sums[rounds : rounds + 1])
+    spot = lax.broadcasted_iota(jnp.int32, (tall, rows), 1)
+    slot = lax.broadcasted_iota(jnp.int32, (tall, rows), 0)
+    out_ref[2:3] = jnp.sum(jnp.where(spot == slot, sums, 0.0), axis=0, keepdims=True)
     for made in sent:
         made.wait_send()
 
@@ -282,20 +307,20 @@
     rounds, total = counts.shape[0], cand_index.shape[3]
     groups, width = lax.axis_size("dp"), lax.axis_size("shard")
     each, classes = total // width, groups // QUAD
-    chunks, tall = 2, 8
+    chunks, tall = 4, 8
     f32, held = jnp.float32, points.dtype
     dma = pltpu.SemaphoreType.DMA
     vmem = pl.BlockSpec(memory_space=pltpu.VMEM)
-    running, weights, potentials = pl.pallas_call(
+    hbm = pl.BlockSpec(memory_space=pltpu.HBM)
+    out = pl.pallas_call(
         functools.partial(round_kernel, groups, width),
-        out_shape=(
-            jax.ShapeDtypeStruct((1, rows), f32),
-            jax.ShapeDtypeStruct((1, rows), f32),
-            jax.ShapeDtypeStruct((rounds + 1,), f32),
-        ),
-        in_specs=[pl.BlockSpec(memory_space=pl.ANY), vmem, vmem, vmem],
-        out_specs=(vmem, vmem, pl.BlockSpec(memory_space=pltpu.SMEM)),
+        out_shape=jax.ShapeDtypeStruct((3, rows), f32),
+        in_specs=[hbm] * 4,
+        out_specs=vmem,
         scratch_shapes=[
+            pltpu.VMEM((depth,), held),
+            pltpu.SMEM((rounds,), counts.dtype),
+            pltpu.VMEM(cand_index.shape, cand_index.dtype),
             pltpu.VMEM((QUAD, rows, depth), held),
             pltpu.VMEM((rounds, width, each, depth), held),
             pltpu.VMEM((rounds, width, each, depth), held),
@@ -304,7 +329,7 @@
             pltpu.VMEM((QUAD, tall, rows), f32),
             pltpu.VMEM((width, tall, LANES), f32),
             pltpu.VMEM((groups, tall, LANES), f32),
-            dma,
+            dma((4,)),
             dma((rounds, width - 1)),
             dma((rounds, width - 1)),
             dma((rounds, classes, width - 1)),
@@ -325,15 +350,15 @@
             dma((groups - 1,)),
         ],
         compiler_params=pltpu.CompilerParams(
-            collective_id=0, has_side_effects=True, vmem_limit_bytes=40 * 1024 * 1024
+            collective_id=0, has_side_effects=True, vmem_limit_bytes=62 * 1024 * 1024
         ),
     )(
         points,
-        first_center.reshape(1, depth),
-        counts.reshape(rounds, 1),
-        cand_index.reshape(rounds, total),
+        first_center,
+        counts.reshape(rounds),
+        cand_index,
     )
-    return running.reshape(rows), weights.reshape(rows), potentials
+    return out[0], out[1], out[2, : rounds + 1]
 
 
 def one_holder(points, counts, cand_index):

time: 44.5 us -> 40.6 us (0.912)
  local copies, waits for them, and re-layouts: 4.69 us -> 2.5 us
  Pallas kernels: 39 us -> 37.2 us
    unnamed x12 -> x0, local copies, waits for them, and re-layouts: 4.6 us -> none
    pallas_call x1, Pallas kernels: 39 us -> 37.2 us  [fused(): pl.pallas_call(functools.partial(round_kernel, groups, width), out_shape=...]
    slice x0 -> x1, local copies, waits for them, and re-layouts: none -> 1.32 us  [fused(): return (out[0], out[1], out[2, :rounds + 1])]
    squeeze x0 -> x1, local copies, waits for them, and re-layouts: none -> 1.18 us  [fused(): return (out[0], out[1], out[2, :rounds + 1])]
where the time goes in v2:
time: 40.6 us; the launch traced here: 40.4 us
  Pallas kernels  37.2 us (92%)
  local copies, waits for them, and re-layouts  2.5 us (6%)
  between operations  0.64 us (2%)
    pallas_call x1, Pallas kernels, fused(): pl.pallas_call(functools.partial(round_kernel, groups, width), out_shape=...  37.2 us
    slice x1, local copies, waits for them, and re-layouts, fused(): return (out[0], out[1], out[2, :rounds + 1])  1.32 us
    squeeze x1, local copies, waits for them, and re-layouts, fused(): return (out[0], out[1], out[2, :rounds + 1])  1.18 us

profile of v2, /device:TPU:0, one launch (start us, length us, event | category | flops | bytes accessed | tf_op | source)
XLA Modules:
  0.0 40.4 jit_solution(18235526311122514528)
XLA Ops:
  0.6 37.2 %shard_map.67 = f32[3,256]{1,0:T(4,128)} custom-call(bf16[256,1024]{1,0:T(8,128)(2,1)} %pts_hbm.1, bf16[1024]{0:T(1024)(128)(2,1)} %fc_hbm.1, s32[3]{0:T(128)} %bitcast.7, s32[3,1,1,64]{3,2,1,0:T(1,128)} %idx_hbm.1), custom_call_target="tpu_custom_call" | custom-call | tf_op jit(solution)/shard_map/pallas_call | solution.py:315
  37.9 1.3 %fusion = (f32[1,256]{1,0:T(1,128)}, f32[1,256]{1,0:T(1,128)}) fusion(f32[3,256]{1,0:T(4,128)} %shard_map.67), kind=kLoop, calls=%fused_computation.1 | loop fusion | bytes 4096 | tf_op jit(solution)/shard_map/slice | solution.py:361
  39.2 1.2 %slice_bitcast_fusion = f32[4]{0:T(128)} fusion(f32[3,256]{1,0:T(4,128)} %shard_map.67), kind=kLoop, calls=%fused_computation | loop fusion | bytes 32 | tf_op jit(solution)/shard_map/squeeze | solution.py:361

commit v3 on v2

--- a/solution.py
+++ b/solution.py
@@ -113,9 +113,13 @@
     for load in loads:
         load.wait()
 
-    def pick(t):
-        spot = lax.broadcasted_iota(jnp.int32, (rows, total), 0)
-        slot = lax.broadcasted_iota(jnp.int32, (rows, total), 1)
+    def cross(j):
+        span = pl.ds(j * chunk, chunk)
+        copy(pts_hbm.at[span], pts.at[mine, span], z_send.at[j], z_recv.at[j], in_quad(across))
+
+    spot = lax.broadcasted_iota(jnp.int32, (rows, total), 0)
+    slot = lax.broadcasted_iota(jnp.int32, (rows, total), 1)
+    for t in range(rounds):
         hit = (spot == idx_ref[t, 0]) & (slot < cnt_ref[t])
         chosen = lax.dot_general(
             jnp.where(hit, 1.0, 0.0).astype(pts.dtype),
@@ -123,30 +127,17 @@
             CONTRACT_FIRST,
             preferred_element_type=jnp.float32,
         )
-        packed[t] = chosen.astype(packed.dtype).reshape(width, each, depth)
-
-    def scatter(t):
-        for off in range(1, width):
-            copy(
-                packed.at[t, lax.rem(me + off, width)],
-                parts.at[t, me],
-                part_send.at[t, off - 1],
-                part_recv.at[t, off - 1],
-                in_plane(off),
-            )
-
-    pick(0)
+        packed[:, t] = chosen.astype(packed.dtype).reshape(width, each, depth)
     pl.semaphore_wait(barrier, width - 1 + groups - 1)
-    scatter(0)
-
-    def cross(j):
-        span = pl.ds(j * chunk, chunk)
-        copy(pts_hbm.at[span], pts.at[mine, span], z_send.at[j], z_recv.at[j], in_quad(across))
-
+    for off in range(1, width):
+        copy(
+            packed.at[lax.rem(me + off, width)],
+            parts.at[me],
+            part_send.at[off - 1],
+            part_recv.at[off - 1],
+            in_plane(off),
+        )
     cross(0)
-    for t in range(1, rounds):
-        pick(t)
-        scatter(t)
     copy(pts_hbm, pts.at[mine], core_send, core_recv, in_quad(partner))
 
     squares = jnp.square(pts[mine].astype(jnp.float32))
@@ -164,93 +155,92 @@
     )[:1]
     running = jnp.maximum(rows_norm + first_norm - 2.0 * first_prod, 0.0)
 
-    def spread(t, c, at):
+    def spread(c, at):
         for off in range(1, width):
             copy(
-                cand.at[t, c, me],
-                cand.at[t, c, me],
-                plane_send.at[t, at, off - 1],
-                plane_recv.at[t, at, off - 1],
+                cand.at[c, me],
+                cand.at[c, me],
+                plane_send.at[at, off - 1],
+                plane_recv.at[at, off - 1],
                 in_plane(off),
             )
 
-    for t in range(rounds):
-        held = packed[t, me].astype(jnp.float32)
+    held = packed[me].astype(jnp.float32)
+    for off in range(1, width):
+        source = lax.rem(me - off + width, width)
+        arrived(parts.at[source], part_send.at[off - 1], part_recv.at[off - 1])
+        held = held + parts[source].astype(jnp.float32)
+    cand[cls, me] = held.astype(cand.dtype)
+    for off in range(1, classes):
+        copy(
+            cand.at[cls, me],
+            cand.at[cls, me],
+            class_send.at[off - 1],
+            class_recv.at[off - 1],
+            in_class(off),
+        )
+    spread(cls, 0)
+    for j in range(1, chunks):
+        cross(j)
+    for off in range(1, classes):
+        source = lax.rem(cls - off + classes, classes)
+        arrived(cand.at[source, me], class_send.at[off - 1], class_recv.at[off - 1])
+        spread(source, off)
+
+    def centers(c):
+        return cand[c].reshape(width * rounds * each, depth)
+
+    def center_norms(c):
+        return jnp.sum(jnp.square(centers(c).astype(jnp.float32)), axis=1, keepdims=True)
+
+    def least(c, norms, k, lo, size):
+        prod = lax.dot_general(
+            centers(c), pts[k, lo : lo + size], CONTRACT_LAST, preferred_element_type=jnp.float32
+        )
+        dist = (norms - 2.0 * prod).reshape(width, rounds, each, size)
+        return jnp.min(jnp.min(dist, axis=0), axis=1)
+
+    def keep(k, lo, found):
+        least_out[k, 0:rounds, lo : lo + found.shape[1]] = found
+
+    def give(k, at):
+        copy(least_out.at[k], least_in.at[mine], least_send.at[at], least_recv.at[at], in_quad(k))
+
+    least_out[...] = jnp.zeros_like(least_out)
+    near_parts = {}
+    norms = []
+    turn = [lax.rem(cls - at + classes, classes) for at in range(classes)]
+    for at, c in enumerate(turn):
         for off in range(1, width):
             source = lax.rem(me - off + width, width)
-            arrived(parts.at[t, source], part_send.at[t, off - 1], part_recv.at[t, off - 1])
-            held = held + parts[t, source].astype(jnp.float32)
-        cand[t, cls, me] = held.astype(cand.dtype)
-        for off in range(1, classes):
-            copy(
-                cand.at[t, cls, me],
-                cand.at[t, cls, me],
-                class_send.at[t, off - 1],
-                class_recv.at[t, off - 1],
-                in_class(off),
-            )
-        spread(t, cls, 0)
-        for j in range(1 + t * (chunks - 1) // rounds, 1 + (t + 1) * (chunks - 1) // rounds):
-            cross(j)
-    for t in range(rounds):
-        for off in range(1, classes):
-            source = lax.rem(cls - off + classes, classes)
-            arrived(cand.at[t, source, me], class_send.at[t, off - 1], class_recv.at[t, off - 1])
-            spread(t, source, off)
-
-    norms = []
-
-    def centers(t):
-        return cand[t].reshape(classes * width * each, depth)
-
-    def least(t, k, lo, size):
-        prod = lax.dot_general(
-            centers(t), pts[k, lo : lo + size], CONTRACT_LAST, preferred_element_type=jnp.float32
-        )
-        least_out[k, t : t + 1, lo : lo + size] = jnp.min(
-            norms[t] - 2.0 * prod, axis=0, keepdims=True
-        )
-
-    def give(k, at):
-        copy(least_out.at[k], least_in.at[mine], least_send.at[at], least_recv.at[at], in_quad(k))
-
-    least_out[...] = jnp.zeros_like(least_out)
-    arrived(pts.at[partner], core_send, core_recv)
-    for t in range(rounds):
-        for at in range(classes):
-            c = lax.rem(cls - at + classes, classes)
-            for off in range(1, width):
-                source = lax.rem(me - off + width, width)
-                arrived(
-                    cand.at[t, c, source],
-                    plane_send.at[t, at, off - 1],
-                    plane_recv.at[t, at, off - 1],
-                )
-        norms.append(
-            jnp.sum(jnp.square(centers(t).astype(jnp.float32)), axis=1, keepdims=True)
-        )
-        least(t, mine, 0, rows)
-        least(t, partner, 0, rows)
+            arrived(cand.at[c, source], plane_send.at[at, off - 1], plane_recv.at[at, off - 1])
+        norms.append(center_norms(c))
+        if at == 0:
+            arrived(pts.at[partner], core_send, core_recv)
+        for k, name in ((mine, 0), (partner, 1)):
+            found = least(c, norms[at], k, 0, rows)
+            near_parts[name] = found if at == 0 else jnp.minimum(near_parts[name], found)
+    keep(mine, 0, near_parts[0])
+    keep(partner, 0, near_parts[1])
     give(partner, 0)
-    for lo in range(0, rows, LANES):
-        for j in range(lo // chunk, (lo + LANES) // chunk):
-            span = pl.ds(j * chunk, chunk)
-            arrived(pts.at[across, span], z_send.at[j], z_recv.at[j])
-            copy(
-                pts.at[across, span],
-                pts.at[across, span],
-                fwd_send.at[j],
-                fwd_recv.at[j],
-                in_quad(partner),
-            )
-        for t in range(rounds):
-            least(t, across, lo, LANES)
+
+    def least_all(k, lo, size):
+        found = least(turn[0], norms[0], k, lo, size)
+        for at in range(1, classes):
+            found = jnp.minimum(found, least(turn[at], norms[at], k, lo, size))
+        keep(k, lo, found)
+
+    for j in range(chunks):
+        span = pl.ds(j * chunk, chunk)
+        arrived(pts.at[across, span], z_send.at[j], z_recv.at[j])
+        copy(
+            pts.at[across, span], pts.at[across, span], fwd_send.at[j], fwd_recv.at[j], in_quad(partner)
+        )
+    least_all(across, 0, rows)
     give(across, 1)
-    for lo in range(0, rows, LANES):
-        for j in range(lo // chunk, (lo + LANES) // chunk):
-            arrived(pts.at[diagonal, pl.ds(j * chunk, chunk)], fwd_send.at[j], fwd_recv.at[j])
-        for t in range(rounds):
-            least(t, diagonal, lo, LANES)
+    for j in range(chunks):
+        arrived(pts.at[diagonal, pl.ds(j * chunk, chunk)], fwd_send.at[j], fwd_recv.at[j])
+    least_all(diagonal, 0, rows)
     give(diagonal, 2)
 
     near = least_out[mine]
@@ -307,7 +297,7 @@
     rounds, total = counts.shape[0], cand_index.shape[3]
     groups, width = lax.axis_size("dp"), lax.axis_size("shard")
     each, classes = total // width, groups // QUAD
-    chunks, tall = 4, 8
+    chunks, tall = 2, 8
     f32, held = jnp.float32, points.dtype
     dma = pltpu.SemaphoreType.DMA
     vmem = pl.BlockSpec(memory_space=pltpu.VMEM)
@@ -322,20 +312,20 @@
             pltpu.SMEM((rounds,), counts.dtype),
             pltpu.VMEM(cand_index.shape, cand_index.dtype),
             pltpu.VMEM((QUAD, rows, depth), held),
-            pltpu.VMEM((rounds, width, each, depth), held),
-            pltpu.VMEM((rounds, width, each, depth), held),
-            pltpu.VMEM((rounds, classes, width, each, depth), held),
+            pltpu.VMEM((width, rounds, each, depth), held),
+            pltpu.VMEM((width, rounds, each, depth), held),
+            pltpu.VMEM((classes, width, rounds, each, depth), held),
             pltpu.VMEM((QUAD, tall, rows), f32),
             pltpu.VMEM((QUAD, tall, rows), f32),
             pltpu.VMEM((width, tall, LANES), f32),
             pltpu.VMEM((groups, tall, LANES), f32),
             dma((4,)),
-            dma((rounds, width - 1)),
-            dma((rounds, width - 1)),
-            dma((rounds, classes, width - 1)),
-            dma((rounds, classes, width - 1)),
-            dma((rounds, max(classes - 1, 1))),
-            dma((rounds, max(classes - 1, 1))),
+            dma((width - 1,)),
+            dma((width - 1,)),
+            dma((classes, width - 1)),
+            dma((classes, width - 1)),
+            dma((max(classes - 1, 1),)),
+            dma((max(classes - 1, 1),)),
             dma,
             dma,
             dma((chunks,)),

time: 40.6 us -> 38.8 us (0.956)
  Pallas kernels: 37.2 us -> 35.4 us
    pallas_call x1, Pallas kernels: 37.2 us -> 35.4 us  [fused(): pl.pallas_call(functools.partial(round_kernel, groups, width), out_shape=...]
where the time goes in v3:
time: 38.8 us; the launch traced here: 38.6 us
  Pallas kernels  35.4 us (91%)
  local copies, waits for them, and re-layouts  2.5 us (6%)
  between operations  0.64 us (2%)
    pallas_call x1, Pallas kernels, fused(): pl.pallas_call(functools.partial(round_kernel, groups, width), out_shape=...  35.4 us
    slice x1, local copies, waits for them, and re-layouts, fused(): return (out[0], out[1], out[2, :rounds + 1])  1.32 us
    squeeze x1, local copies, waits for them, and re-layouts, fused(): return (out[0], out[1], out[2, :rounds + 1])  1.18 us

profile of v3, /device:TPU:0, one launch (start us, length us, event | category | flops | bytes accessed | tf_op | source)
XLA Modules:
  0.0 38.6 jit_solution(7647936067291123040)
XLA Ops:
  0.6 35.4 %shard_map.67 = f32[3,256]{1,0:T(4,128)} custom-call(bf16[256,1024]{1,0:T(8,128)(2,1)} %pts_hbm.1, bf16[1024]{0:T(1024)(128)(2,1)} %fc_hbm.1, s32[3]{0:T(128)} %bitcast.7, s32[3,1,1,64]{3,2,1,0:T(1,128)} %idx_hbm.1), custom_call_target="tpu_custom_call" | custom-call | tf_op jit(solution)/shard_map/pallas_call | solution.py:305
  36.1 1.3 %fusion = (f32[1,256]{1,0:T(1,128)}, f32[1,256]{1,0:T(1,128)}) fusion(f32[3,256]{1,0:T(4,128)} %shard_map.67), kind=kLoop, calls=%fused_computation.1 | loop fusion | bytes 4096 | tf_op jit(solution)/shard_map/slice | solution.py:351
  37.4 1.2 %slice_bitcast_fusion = f32[4]{0:T(128)} fusion(f32[3,256]{1,0:T(4,128)} %shard_map.67), kind=kLoop, calls=%fused_computation | loop fusion | bytes 32 | tf_op jit(solution)/shard_map/squeeze | solution.py:351

commit v4 on v3

--- a/solution.py
+++ b/solution.py
@@ -33,8 +33,7 @@
     cand,
     least_out,
     least_in,
-    plane_sums,
-    dp_sums,
+    all_sums,
     local_sems,
     part_send,
     part_recv,
@@ -50,10 +49,8 @@
     fwd_recv,
     least_send,
     least_recv,
-    psum_send,
-    psum_recv,
-    dsum_send,
-    dsum_recv,
+    sum_send,
+    sum_recv,
 ):
     rounds, total = idx_ref.shape[0], idx_ref.shape[3]
     rows, depth = pts_hbm.shape
@@ -89,7 +86,7 @@
     sent = []
     in_quad = lambda k: (cls * QUAD + k, me)
     in_plane = lambda off: (dp, lax.rem(me + off, width))
-    in_dp = lambda off: (lax.rem(dp + off, groups), me)
+    anyone = lambda a, b: (lax.rem(dp + a, groups), lax.rem(me + b, width))
     in_class = lambda off: (lax.rem(dp + off * QUAD, groups), me)
 
     loads = [
@@ -106,11 +103,10 @@
     for load in loads:
         load.start()
     barrier = pltpu.get_barrier_semaphore()
-    for off in range(1, width):
-        pl.semaphore_signal(barrier, inc=1, device_id=in_plane(off), device_id_type=MESH)
-    for off in range(1, groups):
-        pl.semaphore_signal(barrier, inc=1, device_id=in_dp(off), device_id_type=MESH)
-    for load in loads:
+    others = [(a, b) for a in range(groups) for b in range(width) if a or b]
+    for a, b in others:
+        pl.semaphore_signal(barrier, inc=1, device_id=anyone(a, b), device_id_type=MESH)
+    for load in loads[:3]:
         load.wait()
 
     def cross(j):
@@ -119,16 +115,16 @@
 
     spot = lax.broadcasted_iota(jnp.int32, (rows, total), 0)
     slot = lax.broadcasted_iota(jnp.int32, (rows, total), 1)
+    hits = [(spot == idx_ref[t, 0]) & (slot < cnt_ref[t]) for t in range(rounds)]
+    chosen = lax.dot_general(
+        jnp.concatenate([jnp.where(hit, 1.0, 0.0) for hit in hits], axis=1).astype(pts.dtype),
+        pts[mine],
+        CONTRACT_FIRST,
+        preferred_element_type=jnp.float32,
+    ).astype(packed.dtype)
     for t in range(rounds):
-        hit = (spot == idx_ref[t, 0]) & (slot < cnt_ref[t])
-        chosen = lax.dot_general(
-            jnp.where(hit, 1.0, 0.0).astype(pts.dtype),
-            pts[mine],
-            CONTRACT_FIRST,
-            preferred_element_type=jnp.float32,
-        )
-        packed[:, t] = chosen.astype(packed.dtype).reshape(width, each, depth)
-    pl.semaphore_wait(barrier, width - 1 + groups - 1)
+        packed[:, t] = chosen[t * total : (t + 1) * total].reshape(width, each, depth)
+    pl.semaphore_wait(barrier, len(others))
     for off in range(1, width):
         copy(
             packed.at[lax.rem(me + off, width)],
@@ -145,6 +141,7 @@
     for j in range(1, depth // LANES):
         lanes = lanes + squares[:, j * LANES : (j + 1) * LANES]
     rows_norm = jnp.sum(lanes.T, axis=0, keepdims=True)
+    loads[3].wait()
     first = fc_ref[...].reshape(1, depth)
     first_norm = jnp.sum(jnp.square(first.astype(jnp.float32)), axis=1, keepdims=True)
     first_prod = lax.dot_general(
@@ -186,6 +183,15 @@
         source = lax.rem(cls - off + classes, classes)
         arrived(cand.at[source, me], class_send.at[off - 1], class_recv.at[off - 1])
         spread(source, off)
+
+    def forward(j):
+        span = pl.ds(j * chunk, chunk)
+        arrived(pts.at[across, span], z_send.at[j], z_recv.at[j])
+        copy(
+            pts.at[across, span], pts.at[across, span], fwd_send.at[j], fwd_recv.at[j], in_quad(partner)
+        )
+
+    forward(0)
 
     def centers(c):
         return cand[c].reshape(width * rounds * each, depth)
@@ -220,6 +226,9 @@
         for k, name in ((mine, 0), (partner, 1)):
             found = least(c, norms[at], k, 0, rows)
             near_parts[name] = found if at == 0 else jnp.minimum(near_parts[name], found)
+        if at == 0:
+            for j in range(1, chunks):
+                forward(j)
     keep(mine, 0, near_parts[0])
     keep(partner, 0, near_parts[1])
     give(partner, 0)
@@ -230,12 +239,6 @@
             found = jnp.minimum(found, least(turn[at], norms[at], k, lo, size))
         keep(k, lo, found)
 
-    for j in range(chunks):
-        span = pl.ds(j * chunk, chunk)
-        arrived(pts.at[across, span], z_send.at[j], z_recv.at[j])
-        copy(
-            pts.at[across, span], pts.at[across, span], fwd_send.at[j], fwd_recv.at[j], in_quad(partner)
-        )
     least_all(across, 0, rows)
     give(across, 1)
     for j in range(chunks):
@@ -260,29 +263,17 @@
         partials.append(fold(running))
     out_ref[0:1] = running
 
-    tall = plane_sums.shape[1]
+    tall = all_sums.shape[2]
     partials += [jnp.zeros_like(partials[0])] * (tall - len(partials))
-    plane_sums[me] = jnp.concatenate(partials, axis=0)
-    for off in range(1, width):
-        copy(
-            plane_sums.at[me],
-            plane_sums.at[me],
-            psum_send.at[off - 1],
-            psum_recv.at[off - 1],
-            in_plane(off),
-        )
-    for off in range(1, width):
-        source = lax.rem(me - off + width, width)
-        arrived(plane_sums.at[source], psum_send.at[off - 1], psum_recv.at[off - 1])
-    dp_sums[dp] = jnp.sum(plane_sums[...], axis=0)
-    for off in range(1, groups):
-        copy(
-            dp_sums.at[dp], dp_sums.at[dp], dsum_send.at[off - 1], dsum_recv.at[off - 1], in_dp(off)
-        )
-    for off in range(1, groups):
-        source = lax.rem(dp - off + groups, groups)
-        arrived(dp_sums.at[source], dsum_send.at[off - 1], dsum_recv.at[off - 1])
-    sums = jnp.sum(jnp.sum(dp_sums[...], axis=0), axis=1, keepdims=True)
+    all_sums[dp, me] = jnp.concatenate(partials, axis=0)
+    for a, b in others:
+        copy(all_sums.at[dp, me], all_sums.at[dp, me], sum_send.at[a, b], sum_recv.at[a, b], anyone(a, b))
+    for a, b in others:
+        source = (lax.rem(dp - a + groups, groups), lax.rem(me - b + width, width))
+        arrived(all_sums.at[source], sum_send.at[a, b], sum_recv.at[a, b])
+    sums = jnp.sum(
+        jnp.sum(all_sums[...].reshape(groups * width, tall, LANES), axis=0), axis=1, keepdims=True
+    )
     rows_all = rows * groups * width
     out_ref[1:2] = running * (rows_all / sums[rounds : rounds + 1])
     spot = lax.broadcasted_iota(jnp.int32, (tall, rows), 1)
@@ -317,8 +308,7 @@
             pltpu.VMEM((classes, width, rounds, each, depth), held),
             pltpu.VMEM((QUAD, tall, rows), f32),
             pltpu.VMEM((QUAD, tall, rows), f32),
-            pltpu.VMEM((width, tall, LANES), f32),
-            pltpu.VMEM((groups, tall, LANES), f32),
+            pltpu.VMEM((groups, width, tall, LANES), f32),
             dma((4,)),
             dma((width - 1,)),
             dma((width - 1,)),
@@ -334,10 +324,8 @@
             dma((chunks,)),
             dma((QUAD - 1,)),
             dma((QUAD - 1,)),
-            dma((width - 1,)),
-            dma((width - 1,)),
-            dma((groups - 1,)),
-            dma((groups - 1,)),
+            dma((groups, width)),
+            dma((groups, width)),
         ],
         compiler_params=pltpu.CompilerParams(
             collective_id=0, has_side_effects=True, vmem_limit_bytes=62 * 1024 * 1024

time: 38.8 us -> 38.5 us (level)
  no operation moved by 1% of the time
where the time goes in v4:
time: 38.5 us; the launch traced here: 38.2 us
  Pallas kernels  35.1 us (91%)
  local copies, waits for them, and re-layouts  2.5 us (6%)
  between operations  0.64 us (2%)
    pallas_call x1, Pallas kernels, fused(): pl.pallas_call(functools.partial(round_kernel, groups, width), out_shape=...  35.1 us
    slice x1, local copies, waits for them, and re-layouts, fused(): return (out[0], out[1], out[2, :rounds + 1])  1.32 us
    squeeze x1, local copies, waits for them, and re-layouts, fused(): return (out[0], out[1], out[2, :rounds + 1])  1.18 us

profile of v4, /device:TPU:0, one launch (start us, length us, event | category | flops | bytes accessed | tf_op | source)
XLA Modules:
  0.0 38.2 jit_solution(13732352526974009324)
XLA Ops:
  0.6 35.1 %shard_map.67 = f32[3,256]{1,0:T(4,128)} custom-call(bf16[256,1024]{1,0:T(8,128)(2,1)} %pts_hbm.1, bf16[1024]{0:T(1024)(128)(2,1)} %fc_hbm.1, s32[3]{0:T(128)} %bitcast.7, s32[3,1,1,64]{3,2,1,0:T(1,128)} %idx_hbm.1), custom_call_target="tpu_custom_call" | custom-call | tf_op jit(solution)/shard_map/pallas_call | solution.py:296
  35.7 1.3 %fusion = (f32[1,256]{1,0:T(1,128)}, f32[1,256]{1,0:T(1,128)}) fusion(f32[3,256]{1,0:T(4,128)} %shard_map.67), kind=kLoop, calls=%fused_computation.1 | loop fusion | bytes 4096 | tf_op jit(solution)/shard_map/slice | solution.py:339
  37.0 1.2 %slice_bitcast_fusion = f32[4]{0:T(128)} fusion(f32[3,256]{1,0:T(4,128)} %shard_map.67), kind=kLoop, calls=%fused_computation | loop fusion | bytes 32 | tf_op jit(solution)/shard_map/squeeze | solution.py:339

commit v5 on v3

--- a/solution.py
+++ b/solution.py
@@ -11,6 +11,7 @@
 QUAD = 4
 TILE_ROWS = 16
 LANES = 128
+VMEM_GRANT = 62 * 1024 * 1024
 MESH = pl.DeviceIdType.MESH
 CONTRACT_LAST = (((1,), (1,)), ((), ()))
 CONTRACT_FIRST = (((0,), (0,)), ((), ()))
@@ -23,7 +24,9 @@
     fc_hbm,
     cnt_hbm,
     idx_hbm,
-    out_ref,
+    run_ref,
+    wgt_ref,
+    pot_ref,
     fc_ref,
     cnt_ref,
     idx_ref,
@@ -110,7 +113,7 @@
         pl.semaphore_signal(barrier, inc=1, device_id=in_plane(off), device_id_type=MESH)
     for off in range(1, groups):
         pl.semaphore_signal(barrier, inc=1, device_id=in_dp(off), device_id_type=MESH)
-    for load in loads:
+    for load in loads[:3]:
         load.wait()
 
     def cross(j):
@@ -119,15 +122,15 @@
 
     spot = lax.broadcasted_iota(jnp.int32, (rows, total), 0)
     slot = lax.broadcasted_iota(jnp.int32, (rows, total), 1)
+    hits = [(spot == idx_ref[t, 0]) & (slot < cnt_ref[t]) for t in range(rounds)]
+    chosen = lax.dot_general(
+        jnp.concatenate([jnp.where(hit, 1.0, 0.0) for hit in hits], axis=1).astype(pts.dtype),
+        pts[mine],
+        CONTRACT_FIRST,
+        preferred_element_type=jnp.float32,
+    ).astype(packed.dtype)
     for t in range(rounds):
-        hit = (spot == idx_ref[t, 0]) & (slot < cnt_ref[t])
-        chosen = lax.dot_general(
-            jnp.where(hit, 1.0, 0.0).astype(pts.dtype),
-            pts[mine],
-            CONTRACT_FIRST,
-            preferred_element_type=jnp.float32,
-        )
-        packed[:, t] = chosen.astype(packed.dtype).reshape(width, each, depth)
+        packed[:, t] = chosen[t * total : (t + 1) * total].reshape(width, each, depth)
     pl.semaphore_wait(barrier, width - 1 + groups - 1)
     for off in range(1, width):
         copy(
@@ -145,6 +148,7 @@
     for j in range(1, depth // LANES):
         lanes = lanes + squares[:, j * LANES : (j + 1) * LANES]
     rows_norm = jnp.sum(lanes.T, axis=0, keepdims=True)
+    loads[3].wait()
     first = fc_ref[...].reshape(1, depth)
     first_norm = jnp.sum(jnp.square(first.astype(jnp.float32)), axis=1, keepdims=True)
     first_prod = lax.dot_general(
@@ -187,6 +191,15 @@
         arrived(cand.at[source, me], class_send.at[off - 1], class_recv.at[off - 1])
         spread(source, off)
 
+    def forward(j):
+        span = pl.ds(j * chunk, chunk)
+        arrived(pts.at[across, span], z_send.at[j], z_recv.at[j])
+        copy(
+            pts.at[across, span], pts.at[across, span], fwd_send.at[j], fwd_recv.at[j], in_quad(partner)
+        )
+
+    forward(0)
+
     def centers(c):
         return cand[c].reshape(width * rounds * each, depth)
 
@@ -200,48 +213,33 @@
         dist = (norms - 2.0 * prod).reshape(width, rounds, each, size)
         return jnp.min(jnp.min(dist, axis=0), axis=1)
 
-    def keep(k, lo, found):
-        least_out[k, 0:rounds, lo : lo + found.shape[1]] = found
-
     def give(k, at):
         copy(least_out.at[k], least_in.at[mine], least_send.at[at], least_recv.at[at], in_quad(k))
 
     least_out[...] = jnp.zeros_like(least_out)
-    near_parts = {}
-    norms = []
     turn = [lax.rem(cls - at + classes, classes) for at in range(classes)]
+    found = {}
     for at, c in enumerate(turn):
         for off in range(1, width):
             source = lax.rem(me - off + width, width)
             arrived(cand.at[c, source], plane_send.at[at, off - 1], plane_recv.at[at, off - 1])
-        norms.append(center_norms(c))
-        if at == 0:
-            arrived(pts.at[partner], core_send, core_recv)
-        for k, name in ((mine, 0), (partner, 1)):
-            found = least(c, norms[at], k, 0, rows)
-            near_parts[name] = found if at == 0 else jnp.minimum(near_parts[name], found)
-    keep(mine, 0, near_parts[0])
-    keep(partner, 0, near_parts[1])
-    give(partner, 0)
-
-    def least_all(k, lo, size):
-        found = least(turn[0], norms[0], k, lo, size)
-        for at in range(1, classes):
-            found = jnp.minimum(found, least(turn[at], norms[at], k, lo, size))
-        keep(k, lo, found)
-
-    for j in range(chunks):
-        span = pl.ds(j * chunk, chunk)
-        arrived(pts.at[across, span], z_send.at[j], z_recv.at[j])
-        copy(
-            pts.at[across, span], pts.at[across, span], fwd_send.at[j], fwd_recv.at[j], in_quad(partner)
-        )
-    least_all(across, 0, rows)
-    give(across, 1)
-    for j in range(chunks):
-        arrived(pts.at[diagonal, pl.ds(j * chunk, chunk)], fwd_send.at[j], fwd_recv.at[j])
-    least_all(diagonal, 0, rows)
-    give(diagonal, 2)
+        norms = center_norms(c)
+        for name, k in enumerate((mine, partner, across, diagonal)):
+            if at == 0 and name == 1:
+                arrived(pts.at[partner], core_send, core_recv)
+            if at == 0 and name == 2:
+                for j in range(1, chunks):
+                    forward(j)
+            if at == 0 and name == 3:
+                for j in range(chunks):
+                    span = pl.ds(j * chunk, chunk)
+                    arrived(pts.at[diagonal, span], fwd_send.at[j], fwd_recv.at[j])
+            this = least(c, norms, k, 0, rows)
+            found[name] = this if at == 0 else jnp.minimum(found[name], this)
+            if at == classes - 1:
+                least_out[k, 0:rounds] = found[name]
+                if name > 0:
+                    give(k, name - 1)
 
     near = least_out[mine]
     for at, k in enumerate((partner, across, diagonal)):
@@ -258,7 +256,7 @@
     for t in range(rounds):
         running = jnp.minimum(running, jnp.maximum(rows_norm + near[t : t + 1], 0.0))
         partials.append(fold(running))
-    out_ref[0:1] = running
+    run_ref[...] = running
 
     tall = plane_sums.shape[1]
     partials += [jnp.zeros_like(partials[0])] * (tall - len(partials))
@@ -284,12 +282,23 @@
         arrived(dp_sums.at[source], dsum_send.at[off - 1], dsum_recv.at[off - 1])
     sums = jnp.sum(jnp.sum(dp_sums[...], axis=0), axis=1, keepdims=True)
     rows_all = rows * groups * width
-    out_ref[1:2] = running * (rows_all / sums[rounds : rounds + 1])
-    spot = lax.broadcasted_iota(jnp.int32, (tall, rows), 1)
-    slot = lax.broadcasted_iota(jnp.int32, (tall, rows), 0)
-    out_ref[2:3] = jnp.sum(jnp.where(spot == slot, sums, 0.0), axis=0, keepdims=True)
+    wgt_ref[...] = running * (rows_all / sums[rounds : rounds + 1])
+    for t in range(rounds + 1):
+        pot_ref[t] = sums[t, 0]
     for made in sent:
         made.wait_send()
+
+
+def hand_on(*refs):
+    *arrays, sems = refs
+    count = len(arrays) // 2
+    copies = [
+        pltpu.make_async_copy(arrays[j], arrays[count + j], sems.at[j]) for j in range(count)
+    ]
+    for each in copies:
+        each.start()
+    for each in copies:
+        each.wait()
 
 
 def fused(points, first_center, counts, cand_index):
@@ -302,11 +311,15 @@
     dma = pltpu.SemaphoreType.DMA
     vmem = pl.BlockSpec(memory_space=pltpu.VMEM)
     hbm = pl.BlockSpec(memory_space=pltpu.HBM)
-    out = pl.pallas_call(
+    running, weights, potentials = pl.pallas_call(
         functools.partial(round_kernel, groups, width),
-        out_shape=jax.ShapeDtypeStruct((3, rows), f32),
+        out_shape=(
+            jax.ShapeDtypeStruct((1, rows), f32),
+            jax.ShapeDtypeStruct((1, rows), f32),
+            jax.ShapeDtypeStruct((rounds + 1,), f32),
+        ),
         in_specs=[hbm] * 4,
-        out_specs=vmem,
+        out_specs=(vmem, vmem, pl.BlockSpec(memory_space=pltpu.SMEM)),
         scratch_shapes=[
             pltpu.VMEM((depth,), held),
             pltpu.SMEM((rounds,), counts.dtype),
@@ -340,7 +353,7 @@
             dma((groups - 1,)),
         ],
         compiler_params=pltpu.CompilerParams(
-            collective_id=0, has_side_effects=True, vmem_limit_bytes=62 * 1024 * 1024
+            collective_id=0, has_side_effects=True, vmem_limit_bytes=VMEM_GRANT
         ),
     )(
         points,
@@ -348,7 +361,15 @@
         counts.reshape(rounds),
         cand_index,
     )
-    return out[0], out[1], out[2, : rounds + 1]
+    made = (running.reshape(rows), weights.reshape(rows), potentials)
+    return pl.pallas_call(
+        hand_on,
+        out_shape=[jax.ShapeDtypeStruct(part.shape, part.dtype) for part in made],
+        in_specs=[hbm] * len(made),
+        out_specs=[hbm] * len(made),
+        scratch_shapes=[dma((len(made),))],
+        compiler_params=pltpu.CompilerParams(vmem_limit_bytes=VMEM_GRANT),
+    )(*made)
 
 
 def one_holder(points, counts, cand_index):

time: 38.8 us -> 36.2 us (0.933)
  local copies, waits for them, and re-layouts: 2.5 us -> 0 us
    slice x1 -> x0, local copies, waits for them, and re-layouts: 1.32 us -> none  [fused(): return (out[0], out[1], out[2, :rounds + 1])]
    pallas_call x0 -> x1, Pallas kernels: none -> 1.21 us  [fused(): pl.pallas_call(hand_on, out_shape=[jax.ShapeDtypeStruct(part.shape, part....]
    pallas_call x1, Pallas kernels: 35.4 us -> 34.2 us  [fused(): pl.pallas_call(functools.partial(round_kernel, groups, width), out_shape=...]
    squeeze x1 -> x0, local copies, waits for them, and re-layouts: 1.18 us -> none  [fused(): return (out[0], out[1], out[2, :rounds + 1])]
where the time goes in v5:
time: 36.2 us; the launch traced here: 36.1 us
  Pallas kernels  35.4 us (98%)
  between operations  0.64 us (2%)
    pallas_call x1, Pallas kernels, fused(): pl.pallas_call(functools.partial(round_kernel, groups, width), out_shape=...  34.2 us
    pallas_call x1, Pallas kernels, fused(): pl.pallas_call(hand_on, out_shape=[jax.ShapeDtypeStruct(part.shape, part....  1.21 us

profile of v5, /device:TPU:0, one launch (start us, length us, event | category | flops | bytes accessed | tf_op | source)
XLA Modules:
  0.0 36.1 jit_solution(3439886978098723597)
XLA Ops:
  0.6 34.2 %shard_map.67 = (f32[1,256]{1,0:T(1,128)}, f32[1,256]{1,0:T(1,128)}, f32[4]{0:T(128)}) custom-call(bf16[256,1024]{1,0:T(8,128)(2,1)} %pts_hbm.1, bf16[1024]{0:T(1024)(128)(2,1)} %fc_hbm.1, s32[3]{0:T(128)} %bitcast.5, s32[3,1,1,64]{3,2,1,0:T(1,128)} %idx_hbm.1), custom_call_target="tpu_custom_call" | custom-call | tf_op jit(solution)/shard_map/pallas_call | solution.py:314
  34.9 1.2 %shard_map.68 = (f32[256]{0:T(256)}, f32[256]{0:T(256)}, f32[4]{0:T(128)}) custom-call(f32[256]{0:T(256)} %bitcast.3, f32[256]{0:T(256)} %bitcast.4, f32[4]{0:T(128)} %get-tuple-element.8.refs_2_), custom_call_target="tpu_custom_call" | custom-call | tf_op jit(solution)/shard_map/pallas_call | solution.py:365

commit v6 on v5

--- a/solution.py
+++ b/solution.py
@@ -36,8 +36,7 @@
     cand,
     least_out,
     least_in,
-    plane_sums,
-    dp_sums,
+    all_sums,
     local_sems,
     part_send,
     part_recv,
@@ -53,10 +52,8 @@
     fwd_recv,
     least_send,
     least_recv,
-    psum_send,
-    psum_recv,
-    dsum_send,
-    dsum_recv,
+    sum_send,
+    sum_recv,
 ):
     rounds, total = idx_ref.shape[0], idx_ref.shape[3]
     rows, depth = pts_hbm.shape
@@ -92,8 +89,8 @@
     sent = []
     in_quad = lambda k: (cls * QUAD + k, me)
     in_plane = lambda off: (dp, lax.rem(me + off, width))
-    in_dp = lambda off: (lax.rem(dp + off, groups), me)
-    in_class = lambda off: (lax.rem(dp + off * QUAD, groups), me)
+    anyone = lambda a, b: (lax.rem(dp + a * QUAD, groups), lax.rem(me + b, width))
+    in_class = lambda off: anyone(off, 0)
 
     loads = [
         pltpu.make_async_copy(src, dst, local_sems.at[j])
@@ -111,15 +108,21 @@
     barrier = pltpu.get_barrier_semaphore()
     for off in range(1, width):
         pl.semaphore_signal(barrier, inc=1, device_id=in_plane(off), device_id_type=MESH)
-    for off in range(1, groups):
-        pl.semaphore_signal(barrier, inc=1, device_id=in_dp(off), device_id_type=MESH)
-    for load in loads[:3]:
-        load.wait()
+    for k in (partner, across, diagonal):
+        pl.semaphore_signal(barrier, inc=1, device_id=in_quad(k), device_id_type=MESH)
+    for a in range(1, classes):
+        for b in range(width):
+            pl.semaphore_signal(barrier, inc=1, device_id=anyone(a, b), device_id_type=MESH)
 
     def cross(j):
         span = pl.ds(j * chunk, chunk)
         copy(pts_hbm.at[span], pts.at[mine, span], z_send.at[j], z_recv.at[j], in_quad(across))
 
+    pl.semaphore_wait(barrier, classes * width - 1 + QUAD - 1)
+    for j in range(chunks - 1):
+        cross(j)
+    for load in loads[:3]:
+        load.wait()
     spot = lax.broadcasted_iota(jnp.int32, (rows, total), 0)
     slot = lax.broadcasted_iota(jnp.int32, (rows, total), 1)
     hits = [(spot == idx_ref[t, 0]) & (slot < cnt_ref[t]) for t in range(rounds)]
@@ -131,7 +134,6 @@
     ).astype(packed.dtype)
     for t in range(rounds):
         packed[:, t] = chosen[t * total : (t + 1) * total].reshape(width, each, depth)
-    pl.semaphore_wait(barrier, width - 1 + groups - 1)
     for off in range(1, width):
         copy(
             packed.at[lax.rem(me + off, width)],
@@ -140,7 +142,6 @@
             part_recv.at[off - 1],
             in_plane(off),
         )
-    cross(0)
     copy(pts_hbm, pts.at[mine], core_send, core_recv, in_quad(partner))
 
     squares = jnp.square(pts[mine].astype(jnp.float32))
@@ -184,8 +185,7 @@
             in_class(off),
         )
     spread(cls, 0)
-    for j in range(1, chunks):
-        cross(j)
+    cross(chunks - 1)
     for off in range(1, classes):
         source = lax.rem(cls - off + classes, classes)
         arrived(cand.at[source, me], class_send.at[off - 1], class_recv.at[off - 1])
@@ -198,7 +198,8 @@
             pts.at[across, span], pts.at[across, span], fwd_send.at[j], fwd_recv.at[j], in_quad(partner)
         )
 
-    forward(0)
+    for j in range(chunks - 1):
+        forward(j)
 
     def centers(c):
         return cand[c].reshape(width * rounds * each, depth)
@@ -213,10 +214,12 @@
         dist = (norms - 2.0 * prod).reshape(width, rounds, each, size)
         return jnp.min(jnp.min(dist, axis=0), axis=1)
 
-    def give(k, at):
-        copy(least_out.at[k], least_in.at[mine], least_send.at[at], least_recv.at[at], in_quad(k))
-
-    least_out[...] = jnp.zeros_like(least_out)
+    tall = least_out.shape[0]
+    least_out[QUAD * rounds :] = jnp.concatenate(
+        [rows_norm, running]
+        + [jnp.zeros_like(running)] * (tall - QUAD * rounds - 2),
+        axis=0,
+    )
     turn = [lax.rem(cls - at + classes, classes) for at in range(classes)]
     found = {}
     for at, c in enumerate(turn):
@@ -228,8 +231,7 @@
             if at == 0 and name == 1:
                 arrived(pts.at[partner], core_send, core_recv)
             if at == 0 and name == 2:
-                for j in range(1, chunks):
-                    forward(j)
+                forward(chunks - 1)
             if at == 0 and name == 3:
                 for j in range(chunks):
                     span = pl.ds(j * chunk, chunk)
@@ -237,14 +239,14 @@
             this = least(c, norms, k, 0, rows)
             found[name] = this if at == 0 else jnp.minimum(found[name], this)
             if at == classes - 1:
-                least_out[k, 0:rounds] = found[name]
-                if name > 0:
-                    give(k, name - 1)
-
-    near = least_out[mine]
+                least_out[name * rounds : (name + 1) * rounds] = found[name]
+
     for at, k in enumerate((partner, across, diagonal)):
-        arrived(least_in.at[k], least_send.at[at], least_recv.at[at])
-        near = jnp.minimum(near, least_in[k])
+        copy(least_out, least_in.at[at], least_send.at[at], least_recv.at[at], in_quad(k))
+    told = [least_out[...]]
+    for at in range(QUAD - 1):
+        arrived(least_in.at[at], least_send.at[at], least_recv.at[at])
+        told.append(least_in[at])
 
     def fold(row):
         out = row[:, :LANES]
@@ -252,35 +254,45 @@
             out = out + row[:, j * LANES : (j + 1) * LANES]
         return out
 
-    partials = [fold(running)]
-    for t in range(rounds):
-        running = jnp.minimum(running, jnp.maximum(rows_norm + near[t : t + 1], 0.0))
-        partials.append(fold(running))
+    def block_rows(block):
+        near = told[block][0:rounds]
+        for at in range(QUAD):
+            if at == block:
+                continue
+            from_row = (at ^ block) * rounds
+            near = jnp.minimum(near, told[at][from_row : from_row + rounds])
+        norm = told[block][QUAD * rounds : QUAD * rounds + 1]
+        steps = [told[block][QUAD * rounds + 1 : QUAD * rounds + 2]]
+        for t in range(rounds):
+            steps.append(jnp.minimum(steps[-1], jnp.maximum(norm + near[t : t + 1], 0.0)))
+        return steps
+
+    blocks = [block_rows(block) for block in range(QUAD)]
+    running = blocks[0][-1]
     run_ref[...] = running
-
-    tall = plane_sums.shape[1]
-    partials += [jnp.zeros_like(partials[0])] * (tall - len(partials))
-    plane_sums[me] = jnp.concatenate(partials, axis=0)
-    for off in range(1, width):
+    partials = [
+        (fold(blocks[0][t]) + fold(blocks[1][t])) + (fold(blocks[2][t]) + fold(blocks[3][t]))
+        for t in range(rounds + 1)
+    ]
+    partials += [jnp.zeros_like(partials[0])] * (all_sums.shape[2] - len(partials))
+    all_sums[cls, me] = jnp.concatenate(partials, axis=0)
+    others = [(a, b) for a in range(classes) for b in range(width) if a or b]
+    for a, b in others:
         copy(
-            plane_sums.at[me],
-            plane_sums.at[me],
-            psum_send.at[off - 1],
-            psum_recv.at[off - 1],
-            in_plane(off),
-        )
-    for off in range(1, width):
-        source = lax.rem(me - off + width, width)
-        arrived(plane_sums.at[source], psum_send.at[off - 1], psum_recv.at[off - 1])
-    dp_sums[dp] = jnp.sum(plane_sums[...], axis=0)
-    for off in range(1, groups):
-        copy(
-            dp_sums.at[dp], dp_sums.at[dp], dsum_send.at[off - 1], dsum_recv.at[off - 1], in_dp(off)
-        )
-    for off in range(1, groups):
-        source = lax.rem(dp - off + groups, groups)
-        arrived(dp_sums.at[source], dsum_send.at[off - 1], dsum_recv.at[off - 1])
-    sums = jnp.sum(jnp.sum(dp_sums[...], axis=0), axis=1, keepdims=True)
+            all_sums.at[cls, me],
+            all_sums.at[cls, me],
+            sum_send.at[a, b],
+            sum_recv.at[a, b],
+            anyone(a, b),
+        )
+    for a, b in others:
+        source = (lax.rem(cls - a + classes, classes), lax.rem(me - b + width, width))
+        arrived(all_sums.at[source], sum_send.at[a, b], sum_recv.at[a, b])
+    sums = jnp.sum(
+        jnp.sum(all_sums[...].reshape(classes * width, all_sums.shape[2], LANES), axis=0),
+        axis=1,
+        keepdims=True,
+    )
     rows_all = rows * groups * width
     wgt_ref[...] = running * (rows_all / sums[rounds : rounds + 1])
     for t in range(rounds + 1):
@@ -306,7 +318,7 @@
     rounds, total = counts.shape[0], cand_index.shape[3]
     groups, width = lax.axis_size("dp"), lax.axis_size("shard")
     each, classes = total // width, groups // QUAD
-    chunks, tall = 2, 8
+    chunks, tall = 4, (QUAD * rounds + 2 + 7) // 8 * 8
     f32, held = jnp.float32, points.dtype
     dma = pltpu.SemaphoreType.DMA
     vmem = pl.BlockSpec(memory_space=pltpu.VMEM)
@@ -328,10 +340,9 @@
             pltpu.VMEM((width, rounds, each, depth), held),
             pltpu.VMEM((width, rounds, each, depth), held),
             pltpu.VMEM((classes, width, rounds, each, depth), held),
-            pltpu.VMEM((QUAD, tall, rows), f32),
-            pltpu.VMEM((QUAD, tall, rows), f32),
-            pltpu.VMEM((width, tall, LANES), f32),
-            pltpu.VMEM((groups, tall, LANES), f32),
+            pltpu.VMEM((tall, rows), f32),
+            pltpu.VMEM((QUAD - 1, tall, rows), f32),
+            pltpu.VMEM((classes, width, 8, LANES), f32),
             dma((4,)),
             dma((width - 1,)),
             dma((width - 1,)),
@@ -347,10 +358,8 @@
             dma((chunks,)),
             dma((QUAD - 1,)),
             dma((QUAD - 1,)),
-            dma((width - 1,)),
-            dma((width - 1,)),
-            dma((groups - 1,)),
-            dma((groups - 1,)),
+            dma((classes, width)),
+            dma((classes, width)),
         ],
         compiler_params=pltpu.CompilerParams(
             collective_id=0, has_side_effects=True, vmem_limit_bytes=VMEM_GRANT

time: 36.2 us -> 34.9 us (0.964)
  Pallas kernels: 35.4 us -> 34.1 us
    pallas_call x1, Pallas kernels: 34.2 us -> 32.9 us  [fused(): pl.pallas_call(functools.partial(round_kernel, groups, width), out_shape=...]
where the time goes in v6:
time: 34.9 us; the launch traced here: 34.7 us
  Pallas kernels  34.1 us (98%)
  between operations  0.64 us (2%)
    pallas_call x1, Pallas kernels, fused(): pl.pallas_call(functools.partial(round_kernel, groups, width), out_shape=...  32.9 us
    pallas_call x1, Pallas kernels, fused(): pl.pallas_call(hand_on, out_shape=[jax.ShapeDtypeStruct(part.shape, part....  1.21 us

profile of v6, /device:TPU:0, one launch (start us, length us, event | category | flops | bytes accessed | tf_op | source)
XLA Modules:
  0.0 34.7 jit_solution(16256470924677791801)
XLA Ops:
  0.6 32.9 %shard_map.67 = (f32[1,256]{1,0:T(1,128)}, f32[1,256]{1,0:T(1,128)}, f32[4]{0:T(128)}) custom-call(bf16[256,1024]{1,0:T(8,128)(2,1)} %pts_hbm.1, bf16[1024]{0:T(1024)(128)(2,1)} %fc_hbm.1, s32[3]{0:T(128)} %bitcast.5, s32[3,1,1,64]{3,2,1,0:T(1,128)} %idx_hbm.1), custom_call_target="tpu_custom_call" | custom-call | tf_op jit(solution)/shard_map/pallas_call | solution.py:326
  33.5 1.2 %shard_map.68 = (f32[256]{0:T(256)}, f32[256]{0:T(256)}, f32[4]{0:T(128)}) custom-call(f32[256]{0:T(256)} %bitcast.3, f32[256]{0:T(256)} %bitcast.4, f32[4]{0:T(128)} %get-tuple-element.8.refs_2_), custom_call_target="tpu_custom_call" | custom-call | tf_op jit(solution)/shard_map/pallas_call | solution.py:374

commit v7 on v6

--- a/solution.py
+++ b/solution.py
@@ -63,6 +63,7 @@
     chunk = rows // chunks
 
     dp, me = lax.axis_index("dp"), lax.axis_index("shard")
+    pieces = [(0, 1), (1, rounds)] if rounds > 1 else [(0, rounds)]
     cls, mine = dp // QUAD, dp % QUAD
     zside, core = mine // 2, mine % 2
     partner = zside * 2 + (1 - core)
@@ -119,29 +120,32 @@
         copy(pts_hbm.at[span], pts.at[mine, span], z_send.at[j], z_recv.at[j], in_quad(across))
 
     pl.semaphore_wait(barrier, classes * width - 1 + QUAD - 1)
-    for j in range(chunks - 1):
+    early = chunks - len(pieces)
+    for j in range(early):
         cross(j)
     for load in loads[:3]:
         load.wait()
     spot = lax.broadcasted_iota(jnp.int32, (rows, total), 0)
     slot = lax.broadcasted_iota(jnp.int32, (rows, total), 1)
-    hits = [(spot == idx_ref[t, 0]) & (slot < cnt_ref[t]) for t in range(rounds)]
-    chosen = lax.dot_general(
-        jnp.concatenate([jnp.where(hit, 1.0, 0.0) for hit in hits], axis=1).astype(pts.dtype),
-        pts[mine],
-        CONTRACT_FIRST,
-        preferred_element_type=jnp.float32,
-    ).astype(packed.dtype)
-    for t in range(rounds):
-        packed[:, t] = chosen[t * total : (t + 1) * total].reshape(width, each, depth)
-    for off in range(1, width):
-        copy(
-            packed.at[lax.rem(me + off, width)],
-            parts.at[me],
-            part_send.at[off - 1],
-            part_recv.at[off - 1],
-            in_plane(off),
-        )
+    for p, (t0, t1) in enumerate(pieces):
+        hits = [(spot == idx_ref[t, 0]) & (slot < cnt_ref[t]) for t in range(t0, t1)]
+        chosen = lax.dot_general(
+            jnp.concatenate([jnp.where(hit, 1.0, 0.0) for hit in hits], axis=1).astype(pts.dtype),
+            pts[mine],
+            CONTRACT_FIRST,
+            preferred_element_type=jnp.float32,
+        ).astype(packed.dtype)
+        for t in range(t0, t1):
+            at = (t - t0) * total
+            packed[:, t] = chosen[at : at + total].reshape(width, each, depth)
+        for off in range(1, width):
+            copy(
+                packed.at[lax.rem(me + off, width), t0:t1],
+                parts.at[me, t0:t1],
+                part_send.at[p, off - 1],
+                part_recv.at[p, off - 1],
+                in_plane(off),
+            )
     copy(pts_hbm, pts.at[mine], core_send, core_recv, in_quad(partner))
 
     squares = jnp.square(pts[mine].astype(jnp.float32))
@@ -160,36 +164,41 @@
     )[:1]
     running = jnp.maximum(rows_norm + first_norm - 2.0 * first_prod, 0.0)
 
-    def spread(c, at):
+    def spread(c, at, p):
+        t0, t1 = pieces[p]
         for off in range(1, width):
             copy(
-                cand.at[c, me],
-                cand.at[c, me],
-                plane_send.at[at, off - 1],
-                plane_recv.at[at, off - 1],
+                cand.at[c, me, t0:t1],
+                cand.at[c, me, t0:t1],
+                plane_send.at[at, p, off - 1],
+                plane_recv.at[at, p, off - 1],
                 in_plane(off),
             )
 
-    held = packed[me].astype(jnp.float32)
-    for off in range(1, width):
-        source = lax.rem(me - off + width, width)
-        arrived(parts.at[source], part_send.at[off - 1], part_recv.at[off - 1])
-        held = held + parts[source].astype(jnp.float32)
-    cand[cls, me] = held.astype(cand.dtype)
-    for off in range(1, classes):
-        copy(
-            cand.at[cls, me],
-            cand.at[cls, me],
-            class_send.at[off - 1],
-            class_recv.at[off - 1],
-            in_class(off),
-        )
-    spread(cls, 0)
-    cross(chunks - 1)
-    for off in range(1, classes):
-        source = lax.rem(cls - off + classes, classes)
-        arrived(cand.at[source, me], class_send.at[off - 1], class_recv.at[off - 1])
-        spread(source, off)
+    for p, (t0, t1) in enumerate(pieces):
+        held = packed[me, t0:t1].astype(jnp.float32)
+        for off in range(1, width):
+            source = lax.rem(me - off + width, width)
+            arrived(parts.at[source, t0:t1], part_send.at[p, off - 1], part_recv.at[p, off - 1])
+            held = held + parts[source, t0:t1].astype(jnp.float32)
+        cand[cls, me, t0:t1] = held.astype(cand.dtype)
+        for off in range(1, classes):
+            copy(
+                cand.at[cls, me, t0:t1],
+                cand.at[cls, me, t0:t1],
+                class_send.at[p, off - 1],
+                class_recv.at[p, off - 1],
+                in_class(off),
+            )
+        spread(cls, 0, p)
+        cross(early + p)
+    for p, (t0, t1) in enumerate(pieces):
+        for off in range(1, classes):
+            source = lax.rem(cls - off + classes, classes)
+            arrived(
+                cand.at[source, me, t0:t1], class_send.at[p, off - 1], class_recv.at[p, off - 1]
+            )
+            spread(source, off, p)
 
     def forward(j):
         span = pl.ds(j * chunk, chunk)
@@ -225,7 +234,12 @@
     for at, c in enumerate(turn):
         for off in range(1, width):
             source = lax.rem(me - off + width, width)
-            arrived(cand.at[c, source], plane_send.at[at, off - 1], plane_recv.at[at, off - 1])
+            for p, (t0, t1) in enumerate(pieces):
+                arrived(
+                    cand.at[c, source, t0:t1],
+                    plane_send.at[at, p, off - 1],
+                    plane_recv.at[at, p, off - 1],
+                )
         norms = center_norms(c)
         for name, k in enumerate((mine, partner, across, diagonal)):
             if at == 0 and name == 1:
@@ -344,12 +358,12 @@
             pltpu.VMEM((QUAD - 1, tall, rows), f32),
             pltpu.VMEM((classes, width, 8, LANES), f32),
             dma((4,)),
-            dma((width - 1,)),
-            dma((width - 1,)),
-            dma((classes, width - 1)),
-            dma((classes, width - 1)),
-            dma((max(classes - 1, 1),)),
-            dma((max(classes - 1, 1),)),
+            dma((2, width - 1)),
+            dma((2, width - 1)),
+            dma((classes, 2, width - 1)),
+            dma((classes, 2, width - 1)),
+            dma((2, max(classes - 1, 1))),
+            dma((2, max(classes - 1, 1))),
             dma,
             dma,
             dma((chunks,)),

time: 34.9 us -> 34 us (0.974)
  Pallas kernels: 34.1 us -> 33.2 us
    pallas_call x1, Pallas kernels: 32.9 us -> 32 us  [fused(): pl.pallas_call(functools.partial(round_kernel, groups, width), out_shape=...]
where the time goes in v7:
time: 34 us; the launch traced here: 33.9 us
  Pallas kernels  33.2 us (98%)
  between operations  0.64 us (2%)
    pallas_call x1, Pallas kernels, fused(): pl.pallas_call(functools.partial(round_kernel, groups, width), out_shape=...  32 us
    pallas_call x1, Pallas kernels, fused(): pl.pallas_call(hand_on, out_shape=[jax.ShapeDtypeStruct(part.shape, part....  1.21 us

profile of v7, /device:TPU:0, one launch (start us, length us, event | category | flops | bytes accessed | tf_op | source)
XLA Modules:
  0.0 33.9 jit_solution(3716036613869179287)
XLA Ops:
  0.6 32.0 %shard_map.67 = (f32[1,256]{1,0:T(1,128)}, f32[1,256]{1,0:T(1,128)}, f32[4]{0:T(128)}) custom-call(bf16[256,1024]{1,0:T(8,128)(2,1)} %pts_hbm.1, bf16[1024]{0:T(1024)(128)(2,1)} %fc_hbm.1, s32[3]{0:T(128)} %bitcast.5, s32[3,1,1,64]{3,2,1,0:T(1,128)} %idx_hbm.1), custom_call_target="tpu_custom_call" | custom-call | tf_op jit(solution)/shard_map/pallas_call | solution.py:340
  32.7 1.2 %shard_map.68 = (f32[256]{0:T(256)}, f32[256]{0:T(256)}, f32[4]{0:T(128)}) custom-call(f32[256]{0:T(256)} %bitcast.3, f32[256]{0:T(256)} %bitcast.4, f32[4]{0:T(128)} %get-tuple-element.8.refs_2_), custom_call_target="tpu_custom_call" | custom-call | tf_op jit(solution)/shard_map/pallas_call | solution.py:388

commit v8 on v7

--- a/solution.py
+++ b/solution.py
@@ -24,6 +24,9 @@
     fc_hbm,
     cnt_hbm,
     idx_hbm,
+    run_hbm,
+    wgt_hbm,
+    pot_hbm,
     run_ref,
     wgt_ref,
     pot_ref,
@@ -38,6 +41,7 @@
     least_in,
     all_sums,
     local_sems,
+    out_sems,
     part_send,
     part_recv,
     plane_send,
@@ -120,8 +124,7 @@
         copy(pts_hbm.at[span], pts.at[mine, span], z_send.at[j], z_recv.at[j], in_quad(across))
 
     pl.semaphore_wait(barrier, classes * width - 1 + QUAD - 1)
-    early = chunks - len(pieces)
-    for j in range(early):
+    for j in range(chunks - 1):
         cross(j)
     for load in loads[:3]:
         load.wait()
@@ -191,7 +194,7 @@
                 in_class(off),
             )
         spread(cls, 0, p)
-        cross(early + p)
+    cross(chunks - 1)
     for p, (t0, t1) in enumerate(pieces):
         for off in range(1, classes):
             source = lax.rem(cls - off + classes, classes)
@@ -210,50 +213,62 @@
     for j in range(chunks - 1):
         forward(j)
 
-    def centers(c):
-        return cand[c].reshape(width * rounds * each, depth)
-
-    def center_norms(c):
-        return jnp.sum(jnp.square(centers(c).astype(jnp.float32)), axis=1, keepdims=True)
-
-    def least(c, norms, k, lo, size):
-        prod = lax.dot_general(
-            centers(c), pts[k, lo : lo + size], CONTRACT_LAST, preferred_element_type=jnp.float32
-        )
-        dist = (norms - 2.0 * prod).reshape(width, rounds, each, size)
-        return jnp.min(jnp.min(dist, axis=0), axis=1)
-
+    def least(c, t0, t1, names):
+        centers = cand[c, :, t0:t1].reshape(width * (t1 - t0) * each, depth)
+        norms = jnp.sum(jnp.square(centers.astype(jnp.float32)), axis=1, keepdims=True)
+        for name in names:
+            if callable(name):
+                name()
+                continue
+            prod = lax.dot_general(
+                centers, pts[places[name]], CONTRACT_LAST, preferred_element_type=jnp.float32
+            )
+            dist = (norms - 2.0 * prod).reshape(width, t1 - t0, each, rows)
+            this = jnp.min(jnp.min(dist, axis=0), axis=1)
+            for t in range(t0, t1):
+                row = this[t - t0 : t - t0 + 1]
+                old = found.get((name, t))
+                found[name, t] = row if old is None else jnp.minimum(old, row)
+
+    def gathered(at, p):
+        t0, t1 = pieces[p]
+        c = lax.rem(cls - at + classes, classes)
+        for off in range(1, width):
+            source = lax.rem(me - off + width, width)
+            arrived(
+                cand.at[c, source, t0:t1],
+                plane_send.at[at, p, off - 1],
+                plane_recv.at[at, p, off - 1],
+            )
+        return c
+
+    def across_ready():
+        forward(chunks - 1)
+
+    def diagonal_ready():
+        for j in range(chunks):
+            span = pl.ds(j * chunk, chunk)
+            arrived(pts.at[diagonal, span], fwd_send.at[j], fwd_recv.at[j])
+
+    places = (mine, partner, across, diagonal)
+    found = {}
     tall = least_out.shape[0]
     least_out[QUAD * rounds :] = jnp.concatenate(
         [rows_norm, running]
         + [jnp.zeros_like(running)] * (tall - QUAD * rounds - 2),
         axis=0,
     )
-    turn = [lax.rem(cls - at + classes, classes) for at in range(classes)]
-    found = {}
-    for at, c in enumerate(turn):
-        for off in range(1, width):
-            source = lax.rem(me - off + width, width)
-            for p, (t0, t1) in enumerate(pieces):
-                arrived(
-                    cand.at[c, source, t0:t1],
-                    plane_send.at[at, p, off - 1],
-                    plane_recv.at[at, p, off - 1],
-                )
-        norms = center_norms(c)
-        for name, k in enumerate((mine, partner, across, diagonal)):
-            if at == 0 and name == 1:
-                arrived(pts.at[partner], core_send, core_recv)
-            if at == 0 and name == 2:
-                forward(chunks - 1)
-            if at == 0 and name == 3:
-                for j in range(chunks):
-                    span = pl.ds(j * chunk, chunk)
-                    arrived(pts.at[diagonal, span], fwd_send.at[j], fwd_recv.at[j])
-            this = least(c, norms, k, 0, rows)
-            found[name] = this if at == 0 else jnp.minimum(found[name], this)
-            if at == classes - 1:
-                least_out[name * rounds : (name + 1) * rounds] = found[name]
+    for p in range(len(pieces)):
+        c = gathered(0, p)
+    arrived(pts.at[partner], core_send, core_recv)
+    least(c, 0, rounds, (0, 1, across_ready, 2, diagonal_ready, 3))
+    for at in range(1, classes):
+        for p, (t0, t1) in enumerate(pieces):
+            c = gathered(at, p)
+            least(c, t0, t1, range(QUAD))
+    least_out[: QUAD * rounds] = jnp.concatenate(
+        [found[name, t] for name in range(QUAD) for t in range(rounds)], axis=0
+    )
 
     for at, k in enumerate((partner, across, diagonal)):
         copy(least_out, least_in.at[at], least_send.at[at], least_recv.at[at], in_quad(k))
@@ -284,6 +299,11 @@
     blocks = [block_rows(block) for block in range(QUAD)]
     running = blocks[0][-1]
     run_ref[...] = running
+    leaving = [
+        pltpu.make_async_copy(src, dst, out_sems.at[j])
+        for j, (src, dst) in enumerate(((run_ref, run_hbm), (wgt_ref, wgt_hbm), (pot_ref, pot_hbm)))
+    ]
+    leaving[0].start()
     partials = [
         (fold(blocks[0][t]) + fold(blocks[1][t])) + (fold(blocks[2][t]) + fold(blocks[3][t]))
         for t in range(rounds + 1)
@@ -311,8 +331,12 @@
     wgt_ref[...] = running * (rows_all / sums[rounds : rounds + 1])
     for t in range(rounds + 1):
         pot_ref[t] = sums[t, 0]
+    for made in leaving[1:]:
+        made.start()
     for made in sent:
         made.wait_send()
+    for made in leaving:
+        made.wait()
 
 
 def hand_on(*refs):
@@ -335,7 +359,6 @@
     chunks, tall = 4, (QUAD * rounds + 2 + 7) // 8 * 8
     f32, held = jnp.float32, points.dtype
     dma = pltpu.SemaphoreType.DMA
-    vmem = pl.BlockSpec(memory_space=pltpu.VMEM)
     hbm = pl.BlockSpec(memory_space=pltpu.HBM)
     running, weights, potentials = pl.pallas_call(
         functools.partial(round_kernel, groups, width),
@@ -345,8 +368,11 @@
             jax.ShapeDtypeStruct((rounds + 1,), f32),
         ),
         in_specs=[hbm] * 4,
-        out_specs=(vmem, vmem, pl.BlockSpec(memory_space=pltpu.SMEM)),
+        out_specs=[hbm] * 3,
         scratch_shapes=[
+            pltpu.VMEM((1, rows), f32),
+            pltpu.VMEM((1, rows), f32),
+            pltpu.SMEM((rounds + 1,), f32),
             pltpu.VMEM((depth,), held),
             pltpu.SMEM((rounds,), counts.dtype),
             pltpu.VMEM(cand_index.shape, cand_index.dtype),
@@ -358,6 +384,7 @@
             pltpu.VMEM((QUAD - 1, tall, rows), f32),
             pltpu.VMEM((classes, width, 8, LANES), f32),
             dma((4,)),
+            dma((3,)),
             dma((2, width - 1)),
             dma((2, width - 1)),
             dma((classes, 2, width - 1)),

time: 34 us -> 34.1 us (level)
  no operation moved by 1% of the time
where the time goes in v8:
time: 34.1 us; the launch traced here: 33.9 us
  Pallas kernels  33.3 us (98%)
  between operations  0.64 us (2%)
    pallas_call x1, Pallas kernels, fused(): pl.pallas_call(functools.partial(round_kernel, groups, width), out_shape=...  32.1 us
    pallas_call x1, Pallas kernels, fused(): pl.pallas_call(hand_on, out_shape=[jax.ShapeDtypeStruct(part.shape, part....  1.21 us

profile of v8, /device:TPU:0, one launch (start us, length us, event | category | flops | bytes accessed | tf_op | source)
XLA Modules:
  0.0 33.9 jit_solution(8457676858792208271)
XLA Ops:
  0.6 32.1 %shard_map.67 = (f32[1,256]{1,0:T(1,128)}, f32[1,256]{1,0:T(1,128)}, f32[4]{0:T(128)}) custom-call(bf16[256,1024]{1,0:T(8,128)(2,1)} %pts_hbm.1, bf16[1024]{0:T(1024)(128)(2,1)} %fc_hbm.1, s32[3]{0:T(128)} %bitcast.5, s32[3,1,1,64]{3,2,1,0:T(1,128)} %idx_hbm.1), custom_call_target="tpu_custom_call" | custom-call | tf_op jit(solution)/shard_map/pallas_call | solution.py:363
  32.7 1.2 %shard_map.68 = (f32[256]{0:T(256)}, f32[256]{0:T(256)}, f32[4]{0:T(128)}) custom-call(f32[256]{0:T(256)} %bitcast.3, f32[256]{0:T(256)} %bitcast.4, f32[4]{0:T(128)} %get-tuple-element.8.refs_2_), custom_call_target="tpu_custom_call" | custom-call | tf_op jit(solution)/shard_map/pallas_call | solution.py:415

commit v9 on v8

--- a/solution.py
+++ b/solution.py
@@ -74,6 +74,11 @@
     across = (1 - zside) * 2 + core
     diagonal = (1 - zside) * 2 + (1 - core)
 
+    xpeer, ypeer = me + 1 - 2 * (me % 2), (me + 2) % width
+    corner = (xpeer + 2) % width
+    via = xpeer * (1 - core) + ypeer * core
+    onto = ypeer * (1 - core) + xpeer * core
+
     def copy(src, dst, send, recv, to):
         made = pltpu.make_async_remote_copy(
             src_ref=src, dst_ref=dst, send_sem=send, recv_sem=recv, device_id=to, device_id_type=MESH
@@ -193,9 +198,25 @@
                 class_recv.at[p, off - 1],
                 in_class(off),
             )
-        spread(cls, 0, p)
+        for at, peer in enumerate((xpeer, ypeer)):
+            copy(
+                cand.at[cls, me, t0:t1],
+                cand.at[cls, me, t0:t1],
+                plane_send.at[0, p, at],
+                plane_recv.at[0, p, at],
+                (dp, peer),
+            )
     cross(chunks - 1)
     for p, (t0, t1) in enumerate(pieces):
+        for at, peer in enumerate((xpeer, ypeer)):
+            arrived(cand.at[cls, peer, t0:t1], plane_send.at[0, p, at], plane_recv.at[0, p, at])
+        copy(
+            cand.at[cls, via, t0:t1],
+            cand.at[cls, via, t0:t1],
+            plane_send.at[0, p, 2],
+            plane_recv.at[0, p, 2],
+            (dp, onto),
+        )
         for off in range(1, classes):
             source = lax.rem(cls - off + classes, classes)
             arrived(
@@ -233,6 +254,9 @@
     def gathered(at, p):
         t0, t1 = pieces[p]
         c = lax.rem(cls - at + classes, classes)
+        if at == 0:
+            arrived(cand.at[cls, corner, t0:t1], plane_send.at[0, p, 2], plane_recv.at[0, p, 2])
+            return c
         for off in range(1, width):
             source = lax.rem(me - off + width, width)
             arrived(
@@ -429,7 +453,7 @@
     return (
         cand_index.shape[3] == total
         and groups % QUAD == 0
-        and width > 1
+        and width == 4
         and total % (width * TILE_ROWS) == 0
         and rows % (2 * LANES) == 0
         and depth % LANES == 0

time: 34.1 us -> 34.9 us (1.023)
  Pallas kernels: 33.3 us -> 34.1 us
    pallas_call x1, Pallas kernels: 32.1 us -> 32.9 us  [fused(): pl.pallas_call(functools.partial(round_kernel, groups, width), out_shape=...]
where the time goes in v9:
time: 34.9 us; the launch traced here: 34.8 us
  Pallas kernels  34.1 us (98%)
  between operations  0.64 us (2%)
    pallas_call x1, Pallas kernels, fused(): pl.pallas_call(functools.partial(round_kernel, groups, width), out_shape=...  32.9 us
    pallas_call x1, Pallas kernels, fused(): pl.pallas_call(hand_on, out_shape=[jax.ShapeDtypeStruct(part.shape, part....  1.21 us

profile of v9, /device:TPU:0, one launch (start us, length us, event | category | flops | bytes accessed | tf_op | source)
XLA Modules:
  0.0 34.8 jit_solution(17374052754754503409)
XLA Ops:
  0.6 32.9 %shard_map.67 = (f32[1,256]{1,0:T(1,128)}, f32[1,256]{1,0:T(1,128)}, f32[4]{0:T(128)}) custom-call(bf16[256,1024]{1,0:T(8,128)(2,1)} %pts_hbm.1, bf16[1024]{0:T(1024)(128)(2,1)} %fc_hbm.1, s32[3]{0:T(128)} %bitcast.5, s32[3,1,1,64]{3,2,1,0:T(1,128)} %idx_hbm.1), custom_call_target="tpu_custom_call" | custom-call | tf_op jit(solution)/shard_map/pallas_call | solution.py:387
  33.6 1.2 %shard_map.68 = (f32[256]{0:T(256)}, f32[256]{0:T(256)}, f32[4]{0:T(128)}) custom-call(f32[256]{0:T(256)} %bitcast.3, f32[256]{0:T(256)} %bitcast.4, f32[4]{0:T(128)} %get-tuple-element.8.refs_2_), custom_call_target="tpu_custom_call" | custom-call | tf_op jit(solution)/shard_map/pallas_call | solution.py:439

commit v10 on v8

--- a/solution.py
+++ b/solution.py
@@ -67,7 +67,7 @@
     chunk = rows // chunks
 
     dp, me = lax.axis_index("dp"), lax.axis_index("shard")
-    pieces = [(0, 1), (1, rounds)] if rounds > 1 else [(0, rounds)]
+    pieces = [(0, rounds - 1), (rounds - 1, rounds)] if rounds > 1 else [(0, rounds)]
     cls, mine = dp // QUAD, dp % QUAD
     zside, core = mine // 2, mine % 2
     partner = zside * 2 + (1 - core)

time: 34.1 us -> 34.1 us (level)
  no operation moved by 1% of the time
where the time goes in v10:
time: 34.1 us; the launch traced here: 33.9 us
  Pallas kernels  33.3 us (98%)
  between operations  0.64 us (2%)
    pallas_call x1, Pallas kernels, fused(): pl.pallas_call(functools.partial(round_kernel, groups, width), out_shape=...  32.1 us
    pallas_call x1, Pallas kernels, fused(): pl.pallas_call(hand_on, out_shape=[jax.ShapeDtypeStruct(part.shape, part....  1.21 us

profile of v10, /device:TPU:0, one launch (start us, length us, event | category | flops | bytes accessed | tf_op | source)
XLA Modules:
  0.0 33.9 jit_solution(473562207359166875)
XLA Ops:
  0.6 32.1 %shard_map.67 = (f32[1,256]{1,0:T(1,128)}, f32[1,256]{1,0:T(1,128)}, f32[4]{0:T(128)}) custom-call(bf16[256,1024]{1,0:T(8,128)(2,1)} %pts_hbm.1, bf16[1024]{0:T(1024)(128)(2,1)} %fc_hbm.1, s32[3]{0:T(128)} %bitcast.5, s32[3,1,1,64]{3,2,1,0:T(1,128)} %idx_hbm.1), custom_call_target="tpu_custom_call" | custom-call | tf_op jit(solution)/shard_map/pallas_call | solution.py:363
  32.7 1.2 %shard_map.68 = (f32[256]{0:T(256)}, f32[256]{0:T(256)}, f32[4]{0:T(128)}) custom-call(f32[256]{0:T(256)} %bitcast.3, f32[256]{0:T(256)} %bitcast.4, f32[4]{0:T(128)} %get-tuple-element.8.refs_2_), custom_call_target="tpu_custom_call" | custom-call | tf_op jit(solution)/shard_map/pallas_call | solution.py:415
